TPU v7x, 128 devices: a whole 4x4x4 slice. The times are simulated.
128 devices in a mesh: pipe: 8 (over x_hi, z), expert: 16 (over y, x_lo, core).
Axes of the slice: x: 4 (x_hi: 2, x_lo: 2; x = x_hi * 2 + x_lo), y: 4, z: 4, core: 2. Of those that a mesh axis runs over, the one named last changes fastest.
Arguments:
- onward_block_activation: bfloat16 [8, 2048, 4096], P('pipe', 'expert'), may hold values from -40 to 40
- reverse_stored_activation: bfloat16 [8, 2048, 4096], P('pipe', 'expert'), may hold values from -40 to 40
- reverse_result_derivative: bfloat16 [8, 2048, 4096], P('pipe', 'expert'), may hold values from -6 to 6
- onward_specialist_choices: int32 [8, 2048, 2], P('pipe', 'expert'), may hold values from 0 to 15, as said below
- reverse_specialist_choices: int32 [8, 2048, 2], P('pipe', 'expert'), may hold values from 0 to 15, as said below
- onward_mixing_coefficients: float32 [8, 2048, 2], P('pipe', 'expert'), may hold values from 0.1 to 1
- reverse_mixing_coefficients: float32 [8, 2048, 2], P('pipe', 'expert'), may hold values from 0.1 to 1
- quota_table: int32 [8, 16], P('pipe'), may hold values from 16 to 32, as said below
- rescaling_factor_list: float32 [8, 4096], P('pipe'), may hold values from 0.1 to 1.9
- gating_projection_matrix: bfloat16 [8, 16, 4096, 768], P('pipe', 'expert'), may hold values from -0.09375 to 0.09375
- expansion_matrix: bfloat16 [8, 16, 4096, 768], P('pipe', 'expert'), may hold values from -0.09375 to 0.09375
- contraction_matrix: bfloat16 [8, 16, 768, 4096], P('pipe', 'expert'), may hold values from -0.21875 to 0.21875
Outputs:
- fwd_next: bfloat16 [8, 2048, 4096], P('pipe', 'expert')
- grad_next: bfloat16 [8, 2048, 4096], P('pipe', 'expert')
Inputs may be any that keep to these rules, and one draw needn't show every extreme that they name: `onward_specialist_choices`: each row names two different experts. In every section one expert has capacity 32 and is named by 32 or more entries of every aligned block of 128 tokens, in both micro-batches. `reverse_specialist_choices`: each row names two different experts, with the same property as onward_specialist_choices. `quota_table`: in every section one expert has capacity 32.
All inputs are finite; a program needn't handle non-finite values.
Results may differ from a plain program's by a relative error of at most 0.0053.
Values may be sent and summed in bfloat16 or wider, within the bound.
No kernel may reach another device: no remote copies, remote signals or barrier semaphores. Data moves between devices by JAX's collectives and lax.ppermute only.
A program may use at most 128 MiB of HBM per device.

v0:
```python
import jax
import jax.numpy as jnp
from jax import lax
from jax.sharding import PartitionSpec as P

CAP = 32


EPSILON = 1e-06


def passed_along(value, axis, steps):
    count = lax.axis_size(axis)
    pairs = [(source, (source + steps) % count) for source in range(count)]
    return lax.ppermute(value, axis, pairs)


def normalize(rows_in, scaling):
    values = rows_in.astype(jnp.float32)
    inverse = lax.rsqrt(jnp.mean(values * values, axis=-1, keepdims=True) + EPSILON)
    return (values, inverse, (values * inverse * scaling).astype(jnp.bfloat16))


def block_plan(routes, specialist_quota_bounds):
    count = specialist_quota_bounds.shape[0]
    flat_ids = routes.reshape(-1)
    onehot = (flat_ids[:, None] == jnp.arange(count, dtype=jnp.int32)[None, :]).astype(jnp.int32)
    before = jnp.cumsum(onehot, axis=0) - onehot
    rank_in = jnp.sum(before * onehot, axis=1)
    limits = jnp.sum(onehot * specialist_quota_bounds[None, :], axis=1)
    kept_mask = (rank_in < limits).astype(jnp.int32)
    slot_of = jnp.where(kept_mask > 0, flat_ids * CAP + rank_in, count * CAP)
    entries = jnp.arange(flat_ids.shape[0], dtype=jnp.int32)
    slot_entry = jnp.zeros((count * CAP + 1,), jnp.int32).at[slot_of].set(entries)[:-1]
    filled = jnp.zeros((count * CAP + 1,), jnp.int32).at[slot_of].set(1)[:-1]
    return (slot_of.reshape(routes.shape), kept_mask.reshape(routes.shape), slot_entry, filled)


def expert_forward(rows, gate_w, up_w, down_w):
    gate_pre = jnp.dot(rows, gate_w, preferred_element_type=jnp.float32)
    up_pre = jnp.dot(rows, up_w, preferred_element_type=jnp.float32)
    hidden = (jax.nn.silu(gate_pre) * up_pre).astype(jnp.bfloat16)
    return jnp.dot(hidden, down_w, preferred_element_type=jnp.float32).astype(jnp.bfloat16)


def expert_backward(rows, grads, gate_w, up_w, down_w):
    contract = (((1,), (1,)), ((), ()))
    gate_pre = jnp.dot(rows, gate_w, preferred_element_type=jnp.float32)
    up_pre = jnp.dot(rows, up_w, preferred_element_type=jnp.float32)
    hidden_grad = lax.dot_general(grads, down_w, contract, preferred_element_type=jnp.float32)
    sigmoid_gate = jax.nn.sigmoid(gate_pre)
    gate_grad = (
        hidden_grad * up_pre * sigmoid_gate * (1.0 + gate_pre * (1.0 - sigmoid_gate))
    ).astype(jnp.bfloat16)
    up_grad = (hidden_grad * gate_pre * sigmoid_gate).astype(jnp.bfloat16)
    summed = lax.dot_general(gate_grad, gate_w, contract, preferred_element_type=jnp.float32)
    summed = summed + lax.dot_general(up_grad, up_w, contract, preferred_element_type=jnp.float32)
    return summed.astype(jnp.bfloat16)


def on_device(
    onward_block_activation,
    reverse_stored_activation,
    reverse_result_derivative,
    onward_specialist_choices,
    reverse_specialist_choices,
    onward_mixing_coefficients,
    reverse_mixing_coefficients,
    quota_table,
    rescaling_factor_list,
    gating_projection_matrix,
    expansion_matrix,
    contraction_matrix,
):
    scaling = rescaling_factor_list[0]
    gate_w = gating_projection_matrix[0, 0]
    up_w = expansion_matrix[0, 0]
    down_w = contraction_matrix[0, 0]
    specialist_quota_bounds = quota_table[0]
    groups = lax.axis_size("expert")
    top = onward_specialist_choices.shape[2]
    width = onward_block_activation.shape[2]
    slots = specialist_quota_bounds.shape[0] * CAP
    zero_bf = jnp.zeros((), jnp.bfloat16)
    values_f, inverse_f, normed_f = normalize(onward_block_activation[0], scaling)
    values_b, inverse_b, normed_b = normalize(reverse_stored_activation[0], scaling)
    slot_f, kept_f, entry_f, filled_f = block_plan(
        onward_specialist_choices[0], specialist_quota_bounds
    )
    slot_b, kept_b, entry_b, filled_b = block_plan(
        reverse_specialist_choices[0], specialist_quota_bounds
    )
    mask_f = filled_f[:, None] > 0
    mask_b = filled_b[:, None] > 0
    send_f = jnp.where(mask_f, normed_f[entry_f // top], zero_bf).reshape(groups, CAP, width)
    send_b = jnp.where(mask_b, normed_b[entry_b // top], zero_bf).reshape(groups, CAP, width)
    scale_b = reverse_mixing_coefficients[0].reshape(-1)[entry_b]
    grad_rows = (
        scale_b[:, None] * reverse_result_derivative[0][entry_b // top].astype(jnp.float32)
    ).astype(jnp.bfloat16)
    grad_b = jnp.where(mask_b, grad_rows, zero_bf).reshape(groups, CAP, width)
    received = lax.all_to_all(send_f, "expert", split_axis=0, concat_axis=0, tiled=True)
    shape_in = received.shape
    out_f = expert_forward(received.reshape(-1, width), gate_w, up_w, down_w).reshape(shape_in)
    received = (
        lax.all_to_all(send_b, "expert", split_axis=0, concat_axis=0, tiled=True),
        lax.all_to_all(grad_b, "expert", split_axis=0, concat_axis=0, tiled=True),
    )
    shape_in = received[0].shape
    rows = received[0].reshape(-1, width)
    grads = received[1].reshape(-1, width)
    out_b = expert_backward(rows, grads, gate_w, up_w, down_w).reshape(shape_in)
    back_f, back_b = (
        lax.all_to_all(out_f, "expert", split_axis=0, concat_axis=0, tiled=True),
        lax.all_to_all(out_b, "expert", split_axis=0, concat_axis=0, tiled=True),
    )
    table_f = back_f.reshape(slots, width)
    table_b = back_b.reshape(slots, width)
    picked_f = table_f[jnp.minimum(slot_f, slots - 1)]
    coeff_f = onward_mixing_coefficients[0] * kept_f
    summed_f = jnp.sum(coeff_f[..., None] * picked_f.astype(jnp.float32), axis=1)
    block_result_entries = (values_f + summed_f).astype(jnp.bfloat16)
    picked_b = table_b[jnp.minimum(slot_b, slots - 1)]
    normed_grad = jnp.sum(kept_b[..., None] * picked_b.astype(jnp.float32), axis=1)
    scaled = scaling * normed_grad
    inner = jnp.mean(values_b * scaled, axis=-1, keepdims=True)
    block_source_derivative = (
        reverse_result_derivative[0].astype(jnp.float32)
        + inverse_b * scaled
        - values_b * inverse_b * inverse_b * inverse_b * inner
    )
    block_source_derivative = block_source_derivative.astype(jnp.bfloat16)
    fwd_next = passed_along(block_result_entries, "pipe", 1)
    grad_next = passed_along(block_source_derivative, "pipe", -1)
    return (fwd_next[None], grad_next[None])


def solution(mesh):
    in_specs = (
        P("pipe", "expert", None),
        P("pipe", "expert", None),
        P("pipe", "expert", None),
        P("pipe", "expert", None),
        P("pipe", "expert", None),
        P("pipe", "expert", None),
        P("pipe", "expert", None),
        P("pipe", None),
        P("pipe", None),
        P("pipe", "expert", None, None),
        P("pipe", "expert", None, None),
        P("pipe", "expert", None, None),
    )
    out_specs = (P("pipe", "expert", None), P("pipe", "expert", None))
    return jax.shard_map(
        on_device, mesh=mesh, in_specs=in_specs, out_specs=out_specs, check_vma=False
    )
```

profile of v0, /device:TPU:0, one launch (start us, length us, event | category | flops | bytes accessed | tf_op | source)
XLA Modules:
  0.0 442.3 jit_solution(6436337350768933888)
XLA Ops:
  0.6 0.8 copy.16
  1.4 0.1 eq.54
  1.6 0.1 eq.50
  1.7 0.8 copy.20
  2.5 0.1 eq.62
  2.6 0.1 eq.58
  2.8 0.6 reduce-window.14
  3.4 0.2 slice_reduce_fusion.1
  3.6 0.6 reduce-window.16
  4.2 0.2 slice_reduce_fusion
  4.4 0.1 mul.230
  4.7 0.7 select_reduce_fusion
  5.4 1.4 scatter_custom_fusion.3
  6.9 1.5 fusion.30
  8.4 1.5 fusion.34
  9.9 1.6 fusion.25
  11.5 4.4 gather_fusion.4
  15.9 4.3 gather_fusion.3
  20.4 0.1 reshape_squeeze.2
  20.5 3.5 gather_fusion.2
  24.1 1.4 scatter_custom_fusion.2
  25.6 6.1 %broadcast_select_fusion = (bf16[16,32,4096]{2,1,0:T(8,128)(2,1)}, bf16[16,32,4096]{2,1,0:T(8,128)(2,1)S(1)}) fusion(bf16[16,32,4096]{2,1,0:T(8,128)(2,1)} %bitcast.129, pred[16,32]{1,0:T(8,128)(4,1)S(1)} %gt.62, bf16[16,32,4096]{2,1,0:T(8,128)(2,1)} %bitcast.130, f32[16,32]{1,0:T(8,128)S(1)} %mul.231), kind=kLoop, calls=%fused_computation.33 | loop fusion | flops 10485760 | bytes 16779776 | tf_op jit(solution)/shard_map/jit(_where)/select_n | solution.py:96
  31.7 55.7 %all_to_all.25 = bf16[16,32,4096]{2,1,0:T(8,128)(2,1)} all-to-all(bf16[16,32,4096]{2,1,0:T(8,128)(2,1)S(1)} %get-tuple-element.13), channel_id=1, replica_groups=mesh['pipe'=8,'expert'=16] {'expert'}, dimensions={0} | all-to-all | bytes 8388608 | tf_op jit(solution)/shard_map/all_to_all | solution.py:107
  87.4 5.0 %all-to-all-start.3 = ((bf16[16,32,4096]{2,1,0:T(8,128)(2,1)}), bf16[16,32,4096]{2,1,0:T(8,128)(2,1)}, u32[]{:S(2)}, u32[]{:S(2)}) async-start(bf16[16,32,4096]{2,1,0:T(8,128)(2,1)} %get-tuple-element.12), calls=%async_computation.3 | async-start | bytes 8388608 | tf_op jit(solution)/shard_map/all_to_all | solution.py:106
  92.4 8.7 %fusion.1 = f32[512,768]{1,0:T(8,128)} fusion(bf16[512,4096]{1,0:T(8,128)(2,1)} %bitcast.133, bf16[1,1,768,4096]{3,2,1,0:T(8,128)(2,1)} %param.23), kind=kOutput, calls=%fused_computation.13 | convolution fusion | flops 3221225472 | bytes 12058624 | tf_op jit(solution)/shard_map/dot_general | solution.py:50
  101.1 41.7 %all-to-all-done.3 = bf16[16,32,4096]{2,1,0:T(8,128)(2,1)} async-done(((bf16[16,32,4096]{2,1,0:T(8,128)(2,1)}), bf16[16,32,4096]{2,1,0:T(8,128)(2,1)}, u32[]{:S(2)}, u32[]{:S(2)}) %all-to-all-start.3) | async-done | bytes 4194336 | tf_op jit(solution)/shard_map/all_to_all | solution.py:106
  142.7 7.2 %fusion.13 = f32[512,768]{1,0:T(8,128)S(1)} fusion(bf16[512,4096]{1,0:T(8,128)(2,1)} %bitcast.28, bf16[1,1,4096,768]{3,2,1,0:T(8,128)(2,1)} %param.21), kind=kOutput, calls=%fused_computation.25 | convolution fusion | flops 3221225472 | bytes 12058624 | tf_op jit(solution)/shard_map/dot_general | solution.py:48
  150.0 7.9 %multiply_convert_fusion.1 = bf16[512,768]{1,0:T(8,128)(2,1)S(1)} fusion(f32[512,768]{1,0:T(8,128)S(1)} %fusion.13, f32[512,768]{1,0:T(8,128)S(1)} %copy-done.7, bf16[512,4096]{1,0:T(8,128)(2,1)} %bitcast.28, bf16[1,1,4096,768]{3,2,1,0:T(8,128)(2,1)} %param.22), kind=kOutput, calls=%fused_computation.55 | convolution fusion | flops 3225157632 | bytes 14417920 | tf_op jit(solution)/shard_map/dot_general | solution.py:49
  157.8 8.5 %fusion.5 = f32[512,4096]{1,0:T(8,128)} fusion(bf16[1,1,4096,768]{3,2,1,0:T(8,128)(2,1)} %param.22, f32[512,768]{1,0:T(8,128)S(1)} %copy-done.7, f32[512,768]{1,0:T(8,128)S(1)} %fusion.13), kind=kOutput, calls=%fused_computation.17 | convolution fusion | flops 3223584768 | bytes 17825792 | tf_op jit(solution)/shard_map/dot_general | solution.py:57
  166.3 7.2 %add_convert_fusion = bf16[512,4096]{1,0:T(8,128)(2,1)} fusion(f32[512,4096]{1,0:T(8,128)} %fusion.5, bf16[512,768]{1,0:T(8,128)(2,1)S(1)} %multiply_convert_fusion.1, bf16[1,1,4096,768]{3,2,1,0:T(8,128)(2,1)S(1)} %bitcast.150), kind=kOutput, calls=%fused_computation.12 | convolution fusion | flops 3225419776 | bytes 19660800 | tf_op jit(solution)/shard_map/dot_general | solution.py:56
  173.6 4.5 %all-to-all-start.4 = ((bf16[16,32,4096]{2,1,0:T(8,128)(2,1)}), bf16[16,32,4096]{2,1,0:T(8,128)(2,1)}, u32[]{:S(2)}, u32[]{:S(2)}) async-start(bf16[16,32,4096]{2,1,0:T(8,128)(2,1)} %bitcast.131), calls=%async_computation.4 | async-start | bytes 8388608 | tf_op jit(solution)/shard_map/all_to_all | solution.py:115
  178.1 0.1 reduce_sum.110
  178.3 0.1 reduce_sum.111
  178.4 0.1 reshape.421
  178.6 0.1 convert_element_type.169
  178.7 0.1 mul.213
  178.9 1.6 scatter_custom_fusion
  180.5 1.4 scatter_custom_fusion.1
  182.0 46.4 %all-to-all-done.4 = bf16[16,32,4096]{2,1,0:T(8,128)(2,1)} async-done(((bf16[16,32,4096]{2,1,0:T(8,128)(2,1)}), bf16[16,32,4096]{2,1,0:T(8,128)(2,1)}, u32[]{:S(2)}, u32[]{:S(2)}) %all-to-all-start.4) | async-done | bytes 4194336 | tf_op jit(solution)/shard_map/all_to_all | solution.py:115
  228.5 6.6 %gather_fusion.5 = bf16[256,4096]{1,0:T(8,128)(2,1)S(1)} fusion(bf16[512,4096]{1,0:T(8,128)(2,1)} %bitcast.30, s32[1024]{0:T(1024)S(1)} %pad_clamp_fusion), kind=kCustom, calls=%fused_computation.5 | custom fusion | bytes 4195328 | tf_op jit(solution)/shard_map/gather | solution.py:123
  235.1 4.0 reshape.466
  239.1 8.9 %multiply_reduce_fusion = f32[128,4096]{1,0:T(8,128)S(1)} fusion(f32[128,2,4096]{2,1,0:T(2,128)} %reshape.466, f32[128,2]{1,0:T(8,128)S(1)} %convert_element_type.169), kind=kLoop, calls=%fused_computation.31 | loop fusion | flops 1572864 | bytes 6292480 | tf_op jit(solution)/shard_map/reduce_sum | solution.py:124
  248.0 0.4 fusion.35
  248.4 2.2 fusion.29
  250.6 4.3 gather_fusion
  254.9 2.5 broadcast_select_fusion.1
  257.4 53.5 %all_to_all.26 = bf16[16,32,4096]{2,1,0:T(8,128)(2,1)S(1)} all-to-all(bf16[16,32,4096]{2,1,0:T(8,128)(2,1)S(1)} %broadcast_select_fusion.1), channel_id=1, replica_groups=mesh['pipe'=8,'expert'=16] {'expert'}, dimensions={0} | all-to-all | bytes 8388608 | tf_op jit(solution)/shard_map/all_to_all | solution.py:102
  310.9 2.0 copy-done.3
  312.9 5.5 %fusion.15 = f32[512,768]{1,0:T(8,128)S(1)} fusion(bf16[512,4096]{1,0:T(8,128)(2,1)S(1)} %bitcast.134, bf16[1,1,4096,768]{3,2,1,0:T(8,128)(2,1)} %param.21), kind=kOutput, calls=%fused_computation.27 | convolution fusion | flops 3221225472 | bytes 12058624 | tf_op jit(solution)/shard_map/dot_general | solution.py:40
  318.4 16.5 %fusion.17 = bf16[512,4096]{1,0:T(8,128)(2,1)} fusion(bf16[1,1,768,4096]{3,2,1,0:T(8,128)(2,1)} %param.23, f32[512,768]{1,0:T(8,128)S(1)} %fusion.15, bf16[512,4096]{1,0:T(8,128)(2,1)} %bitcast.135, bf16[1,1,4096,768]{3,2,1,0:T(8,128)(2,1)} %param.22), kind=kOutput, calls=%fused_computation.29 | convolution fusion | flops 6446907392 | bytes 22544384 | tf_op jit(solution)/shard_map/dot_general | solution.py:43
  335.0 4.7 %all-to-all-start.1 = ((bf16[16,32,4096]{2,1,0:T(8,128)(2,1)}), bf16[16,32,4096]{2,1,0:T(8,128)(2,1)}, u32[]{:S(2)}, u32[]{:S(2)}) async-start(bf16[16,32,4096]{2,1,0:T(8,128)(2,1)} %bitcast.132), calls=%async_computation.1 | async-start | bytes 8388608 | tf_op jit(solution)/shard_map/all_to_all | solution.py:114
  339.6 0.1 reduce_sum.102
  339.8 0.1 reduce_sum.103
  340.0 0.1 reshape.389
  340.4 6.4 %collective-permute-start.1 = (bf16[128,4096]{1,0:T(8,128)(2,1)}, bf16[128,4096]{1,0:T(8,128)(2,1)}, u32[]{:S(2)}, u32[]{:S(2)}) collective-permute-start(bf16[128,4096]{1,0:T(8,128)(2,1)} %get-tuple-element.8), channel_id=1, source_target_pairs={{0,112},{16,0},{32,16},{48,32},{64,48},{80,64},{96,80},{112,96},{1... | collective-permute-start | bytes 3145736 | tf_op jit(solution)/shard_map/ppermute | solution.py:15
  346.8 43.6 %all-to-all-done.1 = bf16[16,32,4096]{2,1,0:T(8,128)(2,1)} async-done(((bf16[16,32,4096]{2,1,0:T(8,128)(2,1)}), bf16[16,32,4096]{2,1,0:T(8,128)(2,1)}, u32[]{:S(2)}, u32[]{:S(2)}) %all-to-all-start.1) | async-done | bytes 4194336 | tf_op jit(solution)/shard_map/all_to_all | solution.py:114
  390.5 6.6 %gather_fusion.1 = bf16[256,4096]{1,0:T(8,128)(2,1)S(1)} fusion(bf16[512,4096]{1,0:T(8,128)(2,1)} %bitcast.15, s32[1024]{0:T(1024)S(1)} %pad_clamp_fusion.3), kind=kCustom, calls=%fused_computation.1 | custom fusion | bytes 4195328 | tf_op jit(solution)/shard_map/gather | solution.py:119
  397.1 4.0 reshape.465
  401.1 8.7 %multiply_reduce_fusion.1 = f32[128,4096]{1,0:T(8,128)S(1)} fusion(f32[128,2,4096]{2,1,0:T(2,128)} %reshape.465, f32[128,2]{1,0:T(8,128)S(1)} %bitcast_multiply_fusion), kind=kLoop, calls=%fused_computation.32 | loop fusion | flops 1572864 | bytes 6292480 | tf_op jit(solution)/shard_map/reduce_sum | solution.py:121
  409.8 0.3 fusion.33
  410.1 1.5 collective-permute-start
  411.6 27.2 %collective-permute-done = bf16[128,4096]{1,0:T(8,128)(2,1)S(1)} collective-permute-done((bf16[128,4096]{1,0:T(8,128)(2,1)S(1)}, bf16[128,4096]{1,0:T(8,128)(2,1)S(1)}, u32[]{:S(2)}, u32[]{:S(2)}) %collective-permute-start) | collective-permute-done | bytes 1048608 | tf_op jit(solution)/shard_map/ppermute | solution.py:15
  438.9 1.0 copy.31
  439.8 2.3 copy.32
  (57 shorter events, 1.0 us)
Async XLA Ops:
  11.5 4.4 copy-start
  15.9 4.4 copy-start.5
  87.4 55.4 %all-to-all-start.3 = ((bf16[16,32,4096]{2,1,0:T(8,128)(2,1)}), bf16[16,32,4096]{2,1,0:T(8,128)(2,1)}, u32[]{:S(2)}, u32[]{:S(2)}) async-start(bf16[16,32,4096]{2,1,0:T(8,128)(2,1)} %get-tuple-element.12), calls=%async_computation.3 | async-start | bytes 8388608 | tf_op jit(solution)/shard_map/all_to_all | solution.py:106
  142.7 7.2 %copy-start.7 = (f32[512,768]{1,0:T(8,128)S(1)}, f32[512,768]{1,0:T(8,128)}, u32[]{:S(2)}) copy-start(f32[512,768]{1,0:T(8,128)} %fusion.1) | copy-start | bytes 4718596
  142.7 23.6 %slice-start = ((s8[6291456]{0:T(1024)(128)(4,1)}), s8[4194304]{0:T(1024)(128)(4,1)S(1)}, s32[]{:S(2)}) async-start(s8[6291456]{0:T(1024)(128)(4,1)} %bitcast.149), calls=%async_computation.5 | async-start | bytes 8388608
  149.9 16.4 %slice-start.1 = ((s8[6291456]{0:T(1024)(128)(4,1)}), s8[2097152]{0:T(1024)(128)(4,1)S(1)}, s32[]{:S(2)}) async-start(s8[6291456]{0:T(1024)(128)(4,1)} %bitcast.149), calls=%async_computation.6 | async-start | bytes 4194304
  173.6 54.9 %all-to-all-start.4 = ((bf16[16,32,4096]{2,1,0:T(8,128)(2,1)}), bf16[16,32,4096]{2,1,0:T(8,128)(2,1)}, u32[]{:S(2)}, u32[]{:S(2)}) async-start(bf16[16,32,4096]{2,1,0:T(8,128)(2,1)} %bitcast.131), calls=%async_computation.4 | async-start | bytes 8388608 | tf_op jit(solution)/shard_map/all_to_all | solution.py:115
  239.1 8.9 %copy-start.1 = (bf16[1,128,4096]{2,1,0:T(8,128)(2,1)S(1)}, bf16[1,128,4096]{2,1,0:T(8,128)(2,1)}, u32[]{:S(2)}) copy-start(bf16[1,128,4096]{2,1,0:T(8,128)(2,1)} %param.13) | copy-start | bytes 3145732
  239.1 8.9 %copy-start.4 = (f32[1,4096]{1,0:T(1,128)S(1)}, f32[1,4096]{1,0:T(1,128)}, u32[]{:S(2)}) copy-start(f32[1,4096]{1,0:T(1,128)} %param.20) | copy-start | bytes 49156
  239.1 9.3 %copy-start.2 = (bf16[1,128,4096]{2,1,0:T(8,128)(2,1)S(1)}, bf16[1,128,4096]{2,1,0:T(8,128)(2,1)}, u32[]{:S(2)}) copy-start(bf16[1,128,4096]{2,1,0:T(8,128)(2,1)} %param.12) | copy-start | bytes 3145732
  310.9 2.0 copy-start.3
  335.0 5.3 %copy-start.6 = (f32[1,128,2]{1,2,0:T(2,128)S(1)}, f32[1,128,2]{1,2,0:T(2,128)}, u32[]{:S(2)}) copy-start(f32[1,128,2]{1,2,0:T(2,128)} %param.17) | copy-start | bytes 3076
  335.0 55.5 %all-to-all-start.1 = ((bf16[16,32,4096]{2,1,0:T(8,128)(2,1)}), bf16[16,32,4096]{2,1,0:T(8,128)(2,1)}, u32[]{:S(2)}, u32[]{:S(2)}) async-start(bf16[16,32,4096]{2,1,0:T(8,128)(2,1)} %bitcast.132), calls=%async_computation.1 | async-start | bytes 8388608 | tf_op jit(solution)/shard_map/all_to_all | solution.py:114
  340.4 71.2 %collective-permute-start.1 = (bf16[128,4096]{1,0:T(8,128)(2,1)}, bf16[128,4096]{1,0:T(8,128)(2,1)}, u32[]{:S(2)}, u32[]{:S(2)}) collective-permute-start(bf16[128,4096]{1,0:T(8,128)(2,1)} %get-tuple-element.8), channel_id=1, source_target_pairs={{0,112},{16,0},{32,16},{48,32},{64,48},{80,64},{96,80},{112,96},{1... | collective-permute-start | bytes 3145736 | tf_op jit(solution)/shard_map/ppermute | solution.py:15
  410.1 28.8 %collective-permute-start = (bf16[128,4096]{1,0:T(8,128)(2,1)S(1)}, bf16[128,4096]{1,0:T(8,128)(2,1)S(1)}, u32[]{:S(2)}, u32[]{:S(2)}) collective-permute-start(bf16[128,4096]{1,0:T(8,128)(2,1)S(1)} %fusion.33), channel_id=1, source_target_pairs={{0,16},{16,32},{32,48},{48,64},{64,80},{80,96},{96,112},{112,0},{1... | collective-permute-start | bytes 3145736 | tf_op jit(solution)/shard_map/ppermute | solution.py:15
where the time goes:
time: 449 us; the launch traced here: 442 us
  waiting for transfers between devices  159 us (35%)
  blocking collectives  109 us (24%)
  matrix products  61.6 us (14%)
  local copies, waits for them, and re-layouts  53.3 us (12%)
  other arithmetic  35.9 us (8%)
  starting transfers between devices  22.1 us (5%)
    all_to_all x1, blocking collectives, on_device(): lax.all_to_all(grad_b, 'expert', split_axis=0, concat_axis=0, tiled=True)  55.7 us
    all_to_all x1, blocking collectives, on_device(): lax.all_to_all(send_f, 'expert', split_axis=0, concat_axis=0, tiled=True)  53.5 us
    all_to_all x1, waiting for transfers between devices, on_device(): lax.all_to_all(out_b, 'expert', split_axis=0, concat_axis=0, tiled=True)  46.4 us
    all_to_all x1, waiting for transfers between devices, on_device(): lax.all_to_all(out_f, 'expert', split_axis=0, concat_axis=0, tiled=True)  43.6 us
    all_to_all x1, waiting for transfers between devices, on_device(): lax.all_to_all(send_b, 'expert', split_axis=0, concat_axis=0, tiled=True)  41.7 us
    ppermute x2, waiting for transfers between devices, passed_along(): return lax.ppermute(value, axis, pairs)  27.3 us
    dot_general x1, matrix products, expert_forward(): jnp.dot(hidden, down_w, preferred_element_type=jnp.float32)  16.5 us
  transfers between devices with their start and end apart: 5, of which 4 were waited for; matrix products, arithmetic and copies ran while one was open for 7% of the time, Pallas kernels for 0%

commit v1 on v0

v1 whole, which is shorter than its diff:
```python
import jax
import jax.numpy as jnp
from jax import lax
from jax.sharding import PartitionSpec as P

CAP = 32


EPSILON = 1e-06


def passed_along(value, axis, steps):
    count = lax.axis_size(axis)
    pairs = [(source, (source + steps) % count) for source in range(count)]
    return lax.ppermute(value, axis, pairs)


def inverse_rms(values):
    return lax.rsqrt(jnp.mean(values * values, axis=-1, keepdims=True) + EPSILON)


def slot_map(routes, quota):
    count, tokens = quota.shape[0], routes.shape[0]
    chosen = routes.T
    experts = lax.broadcasted_iota(jnp.int32, (count, tokens), 0)
    first = experts == chosen[0][None, :]
    second = experts == chosen[1][None, :]
    named = first.astype(jnp.bfloat16) + second.astype(jnp.bfloat16)
    row = lax.broadcasted_iota(jnp.int32, (tokens, tokens), 0)
    column = lax.broadcasted_iota(jnp.int32, (tokens, tokens), 1)
    before = jnp.dot(
        named, (row < column).astype(jnp.bfloat16), preferred_element_type=jnp.float32
    ).astype(jnp.int32)

    def slot(mask, ranks, ids):
        rank = jnp.sum(jnp.where(mask, ranks, 0), axis=0)
        limit = jnp.sum(jnp.where(mask, quota[:, None], 0), axis=0)
        return jnp.where(rank < limit, ids * CAP + rank, -1)

    slot_first = slot(first, before, chosen[0])
    slot_second = slot(second, before + first.astype(jnp.int32), chosen[1])
    slots = lax.broadcasted_iota(jnp.int32, (count * CAP, tokens), 0)
    return slots == slot_first[None, :], slots == slot_second[None, :]


def weighted(masks, weights):
    return jnp.where(masks[0], weights[:, 0][None, :], 0.0) + jnp.where(
        masks[1], weights[:, 1][None, :], 0.0
    )


def to_slots(masks, rows):
    place = (masks[0] | masks[1]).astype(jnp.bfloat16)
    return jnp.dot(place, rows, preferred_element_type=jnp.float32)


def from_slots(place, table):
    return lax.dot_general(
        place, table, (((0,), (0,)), ((), ())), preferred_element_type=jnp.float32
    )


def exchange(rows):
    return lax.all_to_all(rows, "expert", split_axis=0, concat_axis=0, tiled=True)


def on_device(
    onward_block_activation,
    reverse_stored_activation,
    reverse_result_derivative,
    onward_specialist_choices,
    reverse_specialist_choices,
    onward_mixing_coefficients,
    reverse_mixing_coefficients,
    quota_table,
    rescaling_factor_list,
    gating_projection_matrix,
    expansion_matrix,
    contraction_matrix,
):
    f32, bf16 = jnp.float32, jnp.bfloat16
    contract = (((1,), (1,)), ((), ()))
    scaling = rescaling_factor_list[0]
    gate_w = gating_projection_matrix[0, 0]
    up_w = expansion_matrix[0, 0]
    down_w = contraction_matrix[0, 0]
    quota = quota_table[0]
    masks_b = slot_map(reverse_specialist_choices[0], quota)
    masks_f = slot_map(onward_specialist_choices[0], quota)

    grad_y = reverse_result_derivative[0]
    scale_b = jnp.sum(weighted(masks_b, reverse_mixing_coefficients[0]), axis=1, keepdims=True)
    grads = exchange((scale_b * to_slots(masks_b, grad_y)).astype(bf16))

    values_b = reverse_stored_activation[0].astype(f32)
    inverse_b = inverse_rms(values_b)
    normed_b = (values_b * inverse_b * scaling).astype(bf16)
    rows_b = exchange(to_slots(masks_b, normed_b).astype(bf16))

    values_f = onward_block_activation[0].astype(f32)
    normed_f = (values_f * inverse_rms(values_f) * scaling).astype(bf16)
    rows_f = exchange(to_slots(masks_f, normed_f).astype(bf16))

    hidden_grad = lax.dot_general(grads, down_w, contract, preferred_element_type=f32)
    gate_pre = jnp.dot(rows_b, gate_w, preferred_element_type=f32)
    up_pre = jnp.dot(rows_b, up_w, preferred_element_type=f32)
    sig = jax.nn.sigmoid(gate_pre)
    gate_grad = (hidden_grad * up_pre * sig * (1.0 + gate_pre * (1.0 - sig))).astype(bf16)
    up_grad = (hidden_grad * gate_pre * sig).astype(bf16)
    out_b = lax.dot_general(gate_grad, gate_w, contract, preferred_element_type=f32)
    out_b = out_b + lax.dot_general(up_grad, up_w, contract, preferred_element_type=f32)
    table_b = exchange(out_b.astype(bf16))

    gate_f = jnp.dot(rows_f, gate_w, preferred_element_type=f32)
    up_f = jnp.dot(rows_f, up_w, preferred_element_type=f32)
    hidden = (jax.nn.silu(gate_f) * up_f).astype(bf16)
    out_f = jnp.dot(hidden, down_w, preferred_element_type=f32).astype(bf16)
    table_f = exchange(out_f)

    place_b = (masks_b[0] | masks_b[1]).astype(bf16)
    scaled = scaling * from_slots(place_b, table_b)
    inner = jnp.mean(values_b * scaled, axis=-1, keepdims=True)
    grad = grad_y.astype(f32) + inverse_b * scaled - values_b * (inverse_b * inverse_b * inverse_b * inner)
    grad_next = passed_along(grad.astype(bf16), "pipe", -1)

    place_f = weighted(masks_f, onward_mixing_coefficients[0])
    high = place_f.astype(bf16)
    low = (place_f - high.astype(f32)).astype(bf16)
    summed = from_slots(high, table_f) + from_slots(low, table_f)
    fwd_next = passed_along((values_f + summed).astype(bf16), "pipe", 1)
    return (fwd_next[None], grad_next[None])


def solution(mesh):
    blocks = P("pipe", "expert", None)
    in_specs = (blocks,) * 7 + (P("pipe", None),) * 2 + (P("pipe", "expert", None, None),) * 3
    return jax.shard_map(
        on_device, mesh=mesh, in_specs=in_specs, out_specs=(blocks, blocks), check_vma=False
    )
```

time: 449 us -> 320 us (0.71); the launches traced: 442 us -> 320 us
  blocking collectives: 109 us -> 0 us
  local copies, waits for them, and re-layouts: 53.3 us -> 4.25 us
  waiting for transfers between devices: 159 us -> 193 us
  other arithmetic: 35.9 us -> 2.15 us
  matrix products: 61.6 us -> 86.5 us
  starting transfers between devices: 22.1 us -> 33.3 us
    all_to_all x2 -> x0, blocking collectives: 109 us -> none  [the longest x1 55.7 us: on_device(): lax.all_to_all(grad_b, 'expert', split_axis=0, concat_axis=0, tiled=True)]
    all_to_all x3 -> x5, waiting for transfers between devices: 132 us -> 171 us  [exchange(): lax.all_to_all(rows, 'expert', split_axis=0, concat_axis=0, tiled=True)]
    gather x6 -> x0, local copies, waits for them, and re-layouts: 29.8 us -> none  [the longest x1 6.61 us: on_device(): picked_b = table_b[jnp.minimum(slot_b, slots - 1)]]
    dot_general x7 -> x15, matrix products: 61.6 us -> 86.5 us  [the longest x1 17 us: on_device(): out_f = jnp.dot(hidden, down_w, preferred_element_type=f32).astype(bf16)]
    reduce_sum x6 -> x3, other arithmetic: 21.8 us -> 0.72 us  [the longest x2 0.57 us: inverse_rms(): jnp.mean(values * values, axis=-1, keepdims=True) + EPSILON]
    all_to_all x3 -> x5, starting transfers between devices: 14.2 us -> 24.6 us  [exchange(): lax.all_to_all(rows, 'expert', split_axis=0, concat_axis=0, tiled=True)]
    select_n x8 -> x0, other arithmetic: 8.72 us -> none  [the longest x1 6.1 us: on_device(): jnp.where(mask_b, normed_b[entry_b // top], zero_bf)]
    convert_element_type x4 -> x0, local copies, waits for them, and re-layouts: 8.26 us -> none  [the longest x1 4 us: on_device(): picked_b.astype(jnp.float32)]
  transfers between devices with their start and end apart: 5 -> 7, of which waited for: 4 -> 7; matrix products, arithmetic and copies ran while one was open for 7% -> 26% of each run, Pallas kernels for 0% -> 0%
where the time goes in v1:
time: 320 us
  waiting for transfers between devices  193 us (60%)
  matrix products  86.5 us (27%)
  starting transfers between devices  33.3 us (10%)
  local copies, waits for them, and re-layouts  4.25 us (1%)
    all_to_all x5, waiting for transfers between devices, exchange(): lax.all_to_all(rows, 'expert', split_axis=0, concat_axis=0, tiled=True)  171 us
    all_to_all x5, starting transfers between devices, exchange(): lax.all_to_all(rows, 'expert', split_axis=0, concat_axis=0, tiled=True)  24.6 us
    ppermute x2, waiting for transfers between devices, passed_along(): return lax.ppermute(value, axis, pairs)  21.7 us
    dot_general x1, matrix products, on_device(): out_f = jnp.dot(hidden, down_w, preferred_element_type=f32).astype(bf16)  17 us
    dot_general x3, matrix products, to_slots(): return jnp.dot(place, rows, preferred_element_type=jnp.float32)  11 us
    dot_general x3, matrix products, from_slots(): lax.dot_general(place, table, (((0,), (0,)), ((), ())), preferred_element...  9.39 us
    ppermute x2, starting transfers between devices, passed_along(): return lax.ppermute(value, axis, pairs)  8.74 us
    dot_general x1, matrix products, on_device(): lax.dot_general(grads, down_w, contract, preferred_element_type=f32)  8.66 us
  transfers between devices with their start and end apart: 7, of which 7 were waited for; matrix products, arithmetic and copies ran while one was open for 26% of the time, Pallas kernels for 0%

profile of v1, /device:TPU:0, one launch (start us, length us, event | category | flops | bytes accessed | tf_op | source)
XLA Modules:
  0.0 319.7 jit_solution(4555287267603344161)
XLA Ops:
  0.6 0.8 slice_bitcast_fusion.7
  1.4 0.8 slice_bitcast_fusion.4
  2.1 0.8 slice_bitcast_fusion.1
  2.9 0.1 convolution_convert_fusion.2
  3.0 0.8 select_reduce_fusion.7
  3.9 0.8 fusion.86
  4.6 0.1 add_reduce_fusion
  4.8 4.4 %multiply_convert_fusion = bf16[512,4096]{1,0:T(8,128)(2,1)} fusion(f32[512]{0:T(512)S(1)} %add_reduce_fusion, bf16[1,128,4096]{2,1,0:T(8,128)(2,1)} %param.14, s32[128]{0:T(128)S(1)} %get-tuple-element.26, s32[128]{0:T(128)S(1)} %get-tuple-element.27), kind=kOutput, calls=%fused_computation.1 | convolution fusion | flops 541261824 | bytes 5245952 | tf_op jit(solution)/shard_map/dot_general | solution.py:54
  9.2 0.0 copy-start.1
  9.2 0.0 copy-start.3
  9.2 5.8 %all-to-all-start.2 = ((bf16[16,32,4096]{2,1,0:T(8,128)(2,1)}), bf16[16,32,4096]{2,1,0:T(8,128)(2,1)}, u32[]{:S(2)}, u32[]{:S(2)}) async-start(bf16[16,32,4096]{2,1,0:T(8,128)(2,1)} %bitcast.135), calls=%async_computation.2 | async-start | bytes 8388608 | tf_op jit(solution)/shard_map/all_to_all | solution.py:64
  15.0 0.0 copy-done.1
  15.0 0.3 fusion.23
  15.3 0.0 copy-done.3
  15.3 3.3 %convolution_convert_fusion.1 = bf16[512,4096]{1,0:T(8,128)(2,1)} fusion(bf16[1,128,4096]{2,1,0:T(8,128)(2,1)S(1)} %copy-done.1, f32[4096]{0:T(1024)S(1)} %bitcast.140, f32[128]{0:T(128)S(1)} %add_rsqrt_fusion.1, s32[128]{0:T(128)S(1)} %get-tuple-element.19, s32[128]{0:T(128)S(1)} %get-tuple-element.18), kind=kOutput, calls=%fused_computation.19 | convolution fusion | flops 541261824 | bytes 5260800 | tf_op jit(solution)/shard_map/dot_general | solution.py:54
  18.6 46.8 %all-to-all-done.2 = bf16[16,32,4096]{2,1,0:T(8,128)(2,1)} async-done(((bf16[16,32,4096]{2,1,0:T(8,128)(2,1)}), bf16[16,32,4096]{2,1,0:T(8,128)(2,1)}, u32[]{:S(2)}, u32[]{:S(2)}) %all-to-all-start.2) | async-done | bytes 4194336 | tf_op jit(solution)/shard_map/all_to_all | solution.py:64
  65.4 0.0 copy-start
  65.4 4.7 %all-to-all-start = ((bf16[16,32,4096]{2,1,0:T(8,128)(2,1)}), bf16[16,32,4096]{2,1,0:T(8,128)(2,1)}, u32[]{:S(2)}, u32[]{:S(2)}) async-start(bf16[16,32,4096]{2,1,0:T(8,128)(2,1)} %bitcast.134), calls=%async_computation | async-start | bytes 8388608 | tf_op jit(solution)/shard_map/all_to_all | solution.py:64
  70.1 0.0 copy-done
  70.1 0.3 fusion.26
  70.4 3.3 %convolution_convert_fusion = bf16[512,4096]{1,0:T(8,128)(2,1)} fusion(bf16[1,128,4096]{2,1,0:T(8,128)(2,1)S(1)} %copy-done, f32[128]{0:T(128)S(1)} %add_rsqrt_fusion, f32[4096]{0:T(1024)S(1)} %bitcast.141, s32[128]{0:T(128)S(1)} %get-tuple-element.26, s32[128]{0:T(128)S(1)} %get-tuple-element.27), kind=kOutput, calls=%fused_computation.18 | convolution fusion | flops 541261824 | bytes 5260800 | tf_op jit(solution)/shard_map/dot_general | solution.py:54
  73.7 46.7 %all-to-all-done = bf16[16,32,4096]{2,1,0:T(8,128)(2,1)} async-done(((bf16[16,32,4096]{2,1,0:T(8,128)(2,1)}), bf16[16,32,4096]{2,1,0:T(8,128)(2,1)}, u32[]{:S(2)}, u32[]{:S(2)}) %all-to-all-start) | async-done | bytes 4194336 | tf_op jit(solution)/shard_map/all_to_all | solution.py:64
  120.5 4.7 %all-to-all-start.3 = ((bf16[16,32,4096]{2,1,0:T(8,128)(2,1)}), bf16[16,32,4096]{2,1,0:T(8,128)(2,1)}, u32[]{:S(2)}, u32[]{:S(2)}) async-start(bf16[16,32,4096]{2,1,0:T(8,128)(2,1)} %bitcast.133), calls=%async_computation.3 | async-start | bytes 8388608 | tf_op jit(solution)/shard_map/all_to_all | solution.py:64
  125.2 8.7 %fusion = f32[512,768]{1,0:T(8,128)} fusion(bf16[512,4096]{1,0:T(8,128)(2,1)} %bitcast.43, bf16[1,1,768,4096]{3,2,1,0:T(8,128)(2,1)} %param.23), kind=kOutput, calls=%fused_computation.2 | convolution fusion | flops 3221225472 | bytes 12058624 | tf_op jit(solution)/shard_map/dot_general | solution.py:104
  133.8 8.6 %fusion.14 = f32[512,768]{1,0:T(8,128)} fusion(bf16[512,4096]{1,0:T(8,128)(2,1)} %bitcast.19, bf16[1,1,4096,768]{3,2,1,0:T(8,128)(2,1)} %param.21), kind=kOutput, calls=%fused_computation.16 | convolution fusion | flops 3221225472 | bytes 12058624 | tf_op jit(solution)/shard_map/dot_general | solution.py:114
  142.5 17.0 %fusion.16 = bf16[512,4096]{1,0:T(8,128)(2,1)} fusion(bf16[1,1,768,4096]{3,2,1,0:T(8,128)(2,1)} %param.23, f32[512,768]{1,0:T(8,128)} %fusion.14, bf16[512,4096]{1,0:T(8,128)(2,1)} %bitcast.19, bf16[1,1,4096,768]{3,2,1,0:T(8,128)(2,1)} %param.22), kind=kOutput, calls=%fused_computation.20 | convolution fusion | flops 6446907392 | bytes 22544384 | tf_op jit(solution)/shard_map/dot_general | solution.py:117
  159.5 15.9 %all-to-all-done.3 = bf16[16,32,4096]{2,1,0:T(8,128)(2,1)} async-done(((bf16[16,32,4096]{2,1,0:T(8,128)(2,1)}), bf16[16,32,4096]{2,1,0:T(8,128)(2,1)}, u32[]{:S(2)}, u32[]{:S(2)}) %all-to-all-start.3) | async-done | bytes 4194336 | tf_op jit(solution)/shard_map/all_to_all | solution.py:64
  175.4 4.8 %all-to-all-start.1 = ((bf16[16,32,4096]{2,1,0:T(8,128)(2,1)}), bf16[16,32,4096]{2,1,0:T(8,128)(2,1)}, u32[]{:S(2)}, u32[]{:S(2)}) async-start(bf16[16,32,4096]{2,1,0:T(8,128)(2,1)} %bitcast.137), calls=%async_computation.1 | async-start | bytes 8388608 | tf_op jit(solution)/shard_map/all_to_all | solution.py:64
  180.2 0.0 copy-start.5
  180.2 7.2 %fusion.12 = f32[512,768]{1,0:T(8,128)S(1)} fusion(bf16[512,4096]{1,0:T(8,128)(2,1)} %bitcast.46, bf16[1,1,4096,768]{3,2,1,0:T(8,128)(2,1)} %param.21), kind=kOutput, calls=%fused_computation.14 | convolution fusion | flops 3221225472 | bytes 12058624 | tf_op jit(solution)/shard_map/dot_general | solution.py:105
  187.3 0.0 copy-done.5
  187.3 0.0 slice-start
  187.3 8.6 %fusion.4 = f32[512,4096]{1,0:T(8,128)} fusion(bf16[1,1,4096,768]{3,2,1,0:T(8,128)(2,1)} %param.22, f32[512,768]{1,0:T(8,128)S(1)} %copy-done.5, f32[512,768]{1,0:T(8,128)S(1)} %fusion.12), kind=kOutput, calls=%fused_computation.6 | convolution fusion | flops 3223584768 | bytes 17825792 | tf_op jit(solution)/shard_map/dot_general | solution.py:111
  195.9 0.0 slice-start.1
  195.9 7.9 %multiply_convert_fusion.2 = bf16[512,768]{1,0:T(8,128)(2,1)S(1)} fusion(f32[512,768]{1,0:T(8,128)S(1)} %fusion.12, f32[512,768]{1,0:T(8,128)S(1)} %copy-done.5, bf16[512,4096]{1,0:T(8,128)(2,1)} %bitcast.46, bf16[1,1,4096,768]{3,2,1,0:T(8,128)(2,1)} %param.22), kind=kOutput, calls=%fused_computation.41 | convolution fusion | flops 3225157632 | bytes 14417920 | tf_op jit(solution)/shard_map/dot_general | solution.py:106
  203.8 0.0 slice-done
  203.8 0.0 slice-done.1
  203.9 7.2 %add_convert_fusion = bf16[512,4096]{1,0:T(8,128)(2,1)} fusion(f32[512,4096]{1,0:T(8,128)} %fusion.4, bf16[512,768]{1,0:T(8,128)(2,1)S(1)} %multiply_convert_fusion.2, bf16[1,1,4096,768]{3,2,1,0:T(8,128)(2,1)S(1)} %bitcast.150), kind=kOutput, calls=%fused_computation | convolution fusion | flops 3225419776 | bytes 19660800 | tf_op jit(solution)/shard_map/dot_general | solution.py:110
  211.1 19.2 %all-to-all-done.1 = bf16[16,32,4096]{2,1,0:T(8,128)(2,1)} async-done(((bf16[16,32,4096]{2,1,0:T(8,128)(2,1)}), bf16[16,32,4096]{2,1,0:T(8,128)(2,1)}, u32[]{:S(2)}, u32[]{:S(2)}) %all-to-all-start.1) | async-done | bytes 4194336 | tf_op jit(solution)/shard_map/all_to_all | solution.py:64
  230.3 0.0 copy-start.4
  230.3 4.7 %all-to-all-start.4 = ((bf16[16,32,4096]{2,1,0:T(8,128)(2,1)}), bf16[16,32,4096]{2,1,0:T(8,128)(2,1)}, u32[]{:S(2)}, u32[]{:S(2)}) async-start(bf16[16,32,4096]{2,1,0:T(8,128)(2,1)} %bitcast.136), calls=%async_computation.4 | async-start | bytes 8388608 | tf_op jit(solution)/shard_map/all_to_all | solution.py:64
  235.0 0.0 copy-done.4
  235.0 3.0 fusion.69
  237.9 3.1 fusion.22
  241.1 2.0 collective-permute-start
  243.1 42.2 %all-to-all-done.4 = bf16[16,32,4096]{2,1,0:T(8,128)(2,1)} async-done(((bf16[16,32,4096]{2,1,0:T(8,128)(2,1)}), bf16[16,32,4096]{2,1,0:T(8,128)(2,1)}, u32[]{:S(2)}, u32[]{:S(2)}) %all-to-all-start.4) | async-done | bytes 4194336 | tf_op jit(solution)/shard_map/all_to_all | solution.py:64
  285.3 0.0 copy-start.2
  285.3 3.3 %fusion.29 = (f32[128]{0:T(128)S(1)}, f32[128,4096]{1,0:T(8,128)S(1)}) fusion(bf16[1,128,4096]{2,1,0:T(8,128)(2,1)S(1)} %copy-done, bf16[512,4096]{1,0:T(8,128)(2,1)} %bitcast.48, s32[128]{0:T(128)S(1)} %get-tuple-element.26, s32[128]{0:T(128)S(1)} %get-tuple-element.27, f32[4096]{0:T(1024)S(1)} %bitcast.142), kind=kOutput, calls=%fused_computation.37 | convolution fusion | flops 539164544 | bytes 7357952 | tf_op jit(solution)/shard_map/dot_general | solution.py:58
  288.6 0.0 copy-done.2
  288.7 0.6 fusion.31
  289.3 6.7 %collective-permute-start.1 = (bf16[128,4096]{1,0:T(8,128)(2,1)S(1)}, bf16[128,4096]{1,0:T(8,128)(2,1)S(1)}, u32[]{:S(2)}, u32[]{:S(2)}) collective-permute-start(bf16[128,4096]{1,0:T(8,128)(2,1)S(1)} %fusion.31), channel_id=1, source_target_pairs={{0,112},{16,0},{32,16},{48,32},{64,48},{80,64},{96,80},{112,96},{1... | collective-permute-start | bytes 3145736 | tf_op jit(solution)/shard_map/ppermute | solution.py:15
  296.0 15.2 %collective-permute-done = bf16[128,4096]{1,0:T(8,128)(2,1)S(1)} collective-permute-done((bf16[128,4096]{1,0:T(8,128)(2,1)S(1)}, bf16[128,4096]{1,0:T(8,128)(2,1)S(1)}, u32[]{:S(2)}, u32[]{:S(2)}) %collective-permute-start) | collective-permute-done | bytes 1048608 | tf_op jit(solution)/shard_map/ppermute | solution.py:15
  311.3 6.5 %collective-permute-done.1 = bf16[128,4096]{1,0:T(8,128)(2,1)S(1)} collective-permute-done((bf16[128,4096]{1,0:T(8,128)(2,1)S(1)}, bf16[128,4096]{1,0:T(8,128)(2,1)S(1)}, u32[]{:S(2)}, u32[]{:S(2)}) %collective-permute-start.1) | collective-permute-done | bytes 1048608 | tf_op jit(solution)/shard_map/ppermute | solution.py:15
  317.8 1.0 copy.16
  318.8 1.0 copy.17
  (5 shorter events, 0.0 us)
Async XLA Ops:
  9.2 5.8 %copy-start.1 = (bf16[1,128,4096]{2,1,0:T(8,128)(2,1)S(1)}, bf16[1,128,4096]{2,1,0:T(8,128)(2,1)}, u32[]{:S(2)}) copy-start(bf16[1,128,4096]{2,1,0:T(8,128)(2,1)} %param.12) | copy-start | bytes 3145732
  9.2 6.1 %copy-start.3 = (f32[1,4096]{1,0:T(1,128)S(1)}, f32[1,4096]{1,0:T(1,128)}, u32[]{:S(2)}) copy-start(f32[1,4096]{1,0:T(1,128)} %param.20) | copy-start | bytes 49156
  9.2 56.2 %all-to-all-start.2 = ((bf16[16,32,4096]{2,1,0:T(8,128)(2,1)}), bf16[16,32,4096]{2,1,0:T(8,128)(2,1)}, u32[]{:S(2)}, u32[]{:S(2)}) async-start(bf16[16,32,4096]{2,1,0:T(8,128)(2,1)} %bitcast.135), calls=%async_computation.2 | async-start | bytes 8388608 | tf_op jit(solution)/shard_map/all_to_all | solution.py:64
  65.4 4.7 %copy-start = (bf16[1,128,4096]{2,1,0:T(8,128)(2,1)S(1)}, bf16[1,128,4096]{2,1,0:T(8,128)(2,1)}, u32[]{:S(2)}) copy-start(bf16[1,128,4096]{2,1,0:T(8,128)(2,1)} %param.13) | copy-start | bytes 3145732
  65.4 55.1 %all-to-all-start = ((bf16[16,32,4096]{2,1,0:T(8,128)(2,1)}), bf16[16,32,4096]{2,1,0:T(8,128)(2,1)}, u32[]{:S(2)}, u32[]{:S(2)}) async-start(bf16[16,32,4096]{2,1,0:T(8,128)(2,1)} %bitcast.134), calls=%async_computation | async-start | bytes 8388608 | tf_op jit(solution)/shard_map/all_to_all | solution.py:64
  120.5 54.9 %all-to-all-start.3 = ((bf16[16,32,4096]{2,1,0:T(8,128)(2,1)}), bf16[16,32,4096]{2,1,0:T(8,128)(2,1)}, u32[]{:S(2)}, u32[]{:S(2)}) async-start(bf16[16,32,4096]{2,1,0:T(8,128)(2,1)} %bitcast.133), calls=%async_computation.3 | async-start | bytes 8388608 | tf_op jit(solution)/shard_map/all_to_all | solution.py:64
  175.4 54.9 %all-to-all-start.1 = ((bf16[16,32,4096]{2,1,0:T(8,128)(2,1)}), bf16[16,32,4096]{2,1,0:T(8,128)(2,1)}, u32[]{:S(2)}, u32[]{:S(2)}) async-start(bf16[16,32,4096]{2,1,0:T(8,128)(2,1)} %bitcast.137), calls=%async_computation.1 | async-start | bytes 8388608 | tf_op jit(solution)/shard_map/all_to_all | solution.py:64
  180.2 7.2 %copy-start.5 = (f32[512,768]{1,0:T(8,128)S(1)}, f32[512,768]{1,0:T(8,128)}, u32[]{:S(2)}) copy-start(f32[512,768]{1,0:T(8,128)} %fusion) | copy-start | bytes 4718596
  187.3 16.5 %slice-start = ((s8[6291456]{0:T(1024)(128)(4,1)}), s8[4194304]{0:T(1024)(128)(4,1)S(1)}, s32[]{:S(2)}) async-start(s8[6291456]{0:T(1024)(128)(4,1)} %bitcast.149), calls=%async_computation.5 | async-start | bytes 8388608
  195.9 7.9 %slice-start.1 = ((s8[6291456]{0:T(1024)(128)(4,1)}), s8[2097152]{0:T(1024)(128)(4,1)S(1)}, s32[]{:S(2)}) async-start(s8[6291456]{0:T(1024)(128)(4,1)} %bitcast.149), calls=%async_computation.6 | async-start | bytes 4194304
  230.3 4.7 %copy-start.4 = (f32[1,128,2]{1,2,0:T(2,128)S(1)}, f32[1,128,2]{1,2,0:T(2,128)}, u32[]{:S(2)}) copy-start(f32[1,128,2]{1,2,0:T(2,128)} %param.17) | copy-start | bytes 3076
  230.3 55.0 %all-to-all-start.4 = ((bf16[16,32,4096]{2,1,0:T(8,128)(2,1)}), bf16[16,32,4096]{2,1,0:T(8,128)(2,1)}, u32[]{:S(2)}, u32[]{:S(2)}) async-start(bf16[16,32,4096]{2,1,0:T(8,128)(2,1)} %bitcast.136), calls=%async_computation.4 | async-start | bytes 8388608 | tf_op jit(solution)/shard_map/all_to_all | solution.py:64
  241.1 70.2 %collective-permute-start = (bf16[128,4096]{1,0:T(8,128)(2,1)S(1)}, bf16[128,4096]{1,0:T(8,128)(2,1)S(1)}, u32[]{:S(2)}, u32[]{:S(2)}) collective-permute-start(bf16[128,4096]{1,0:T(8,128)(2,1)S(1)} %fusion.22), channel_id=1, source_target_pairs={{0,16},{16,32},{32,48},{48,64},{64,80},{80,96},{96,112},{112,0},{1... | collective-permute-start | bytes 3145736 | tf_op jit(solution)/shard_map/ppermute | solution.py:15
  285.3 3.3 %copy-start.2 = (bf16[1,128,4096]{2,1,0:T(8,128)(2,1)S(1)}, bf16[1,128,4096]{2,1,0:T(8,128)(2,1)}, u32[]{:S(2)}) copy-start(bf16[1,128,4096]{2,1,0:T(8,128)(2,1)} %param.14) | copy-start | bytes 3145732
  289.3 28.5 %collective-permute-start.1 = (bf16[128,4096]{1,0:T(8,128)(2,1)S(1)}, bf16[128,4096]{1,0:T(8,128)(2,1)S(1)}, u32[]{:S(2)}, u32[]{:S(2)}) collective-permute-start(bf16[128,4096]{1,0:T(8,128)(2,1)S(1)} %fusion.31), channel_id=1, source_target_pairs={{0,112},{16,0},{32,16},{48,32},{64,48},{80,64},{96,80},{112,96},{1... | collective-permute-start | bytes 3145736 | tf_op jit(solution)/shard_map/ppermute | solution.py:15

commit v2 on v1

v2 whole, which is shorter than its diff:
```python
import functools

import jax
import jax.numpy as jnp
from jax import lax
from jax.experimental import pallas as pl
from jax.experimental.pallas import tpu as pltpu
from jax.sharding import PartitionSpec as P

CAP = 32
EPSILON = 1e-06
VMEM_LIMIT = 56 * 1024 * 1024
f32, bf16 = jnp.float32, jnp.bfloat16
ANY = pl.BlockSpec(memory_space=pl.ANY)


def params(steps):
    return pltpu.CompilerParams(
        dimension_semantics=("arbitrary",) * steps, vmem_limit_bytes=VMEM_LIMIT
    )


def cost(flops, moved_bytes):
    return pl.CostEstimate(flops=flops, bytes_accessed=moved_bytes, transcendentals=0)


def whole(shape):
    return pl.BlockSpec(shape, lambda *_: (0,) * len(shape))


def passed_along(value, axis, steps):
    count = lax.axis_size(axis)
    pairs = [(source, (source + steps) % count) for source in range(count)]
    return lax.ppermute(value, axis, pairs)


def inverse_rms(values):
    return lax.rsqrt(jnp.mean(values * values, axis=-1, keepdims=True) + EPSILON)


def after(value, *others):
    return lax.optimization_barrier((value, *others))[0]


def slots_of(chosen, quota):
    count, tokens = quota.shape[0], chosen.shape[1]
    experts = lax.broadcasted_iota(jnp.int32, (count, tokens), 0)
    first = experts == chosen[0][None, :]
    second = experts == chosen[1][None, :]
    named = first.astype(bf16) + second.astype(bf16)
    row = lax.broadcasted_iota(jnp.int32, (tokens, tokens), 0)
    column = lax.broadcasted_iota(jnp.int32, (tokens, tokens), 1)
    before = jnp.dot(
        named, (row < column).astype(bf16), preferred_element_type=f32
    ).astype(jnp.int32)

    def slot(mask, ranks, ids):
        rank = jnp.sum(jnp.where(mask, ranks, 0), axis=0)
        limit = jnp.sum(jnp.where(mask, quota[:, None], 0), axis=0)
        return jnp.where(rank < limit, ids * CAP + rank, -1)

    return jnp.stack(
        [
            slot(first, before, chosen[0]),
            slot(second, before + first.astype(jnp.int32), chosen[1]),
        ]
    )


def masks(place, count):
    rows = lax.broadcasted_iota(jnp.int32, (count, place.shape[1]), 0)
    return rows == place[0:1, :], rows == place[1:2, :]


def dispatch_kernel(place_ref, weight_ref, inverse_ref, scaling_ref, values_ref, grad_ref, out):
    count, rows_each, tile = out.shape
    first, second = masks(place_ref[...], count * CAP)
    chosen = jnp.where(first | second, 1.0, 0.0).astype(bf16)
    normed = values_ref[...].astype(f32) * inverse_ref[...] * scaling_ref[...]
    rows = jnp.dot(chosen, normed.astype(bf16), preferred_element_type=f32)
    out[:, :CAP, :] = rows.astype(bf16).reshape(count, CAP, tile)
    if rows_each > CAP:
        weight = weight_ref[...]
        scale = jnp.where(first, weight[0:1, :], 0.0) + jnp.where(second, weight[1:2, :], 0.0)
        rows = jnp.dot(chosen, grad_ref[...], preferred_element_type=f32)
        rows = rows * jnp.sum(scale, axis=1, keepdims=True)
        out[:, CAP:, :] = rows.astype(bf16).reshape(count, CAP, tile)


def dispatch(count, place, weight, inverse, scaling, values, grad):
    tokens, width = values.shape
    tile = 1024
    rows_each = CAP if grad is None else 2 * CAP
    column = pl.BlockSpec((tokens, tile), lambda i: (0, i))
    return pl.pallas_call(
        dispatch_kernel,
        grid=(width // tile,),
        in_specs=[
            whole(place.shape),
            whole(weight.shape),
            whole(inverse.shape),
            pl.BlockSpec((1, tile), lambda i: (0, i)),
            column,
            column,
        ],
        out_specs=pl.BlockSpec((count, rows_each, tile), lambda i: (0, 0, i)),
        out_shape=jax.ShapeDtypeStruct((count, rows_each, width), bf16),
        compiler_params=params(1),
        cost_estimate=cost(2 * count * rows_each * tokens * width, 2 * (count * rows_each + 2 * tokens) * width),
    )(place, weight, inverse, scaling, values, values if grad is None else grad)


CHUNK = 256


def load(source, start, rows, semaphore):
    copy = pltpu.make_async_copy(source.at[:, pl.ds(start, CAP), :], rows, semaphore)
    copy.start()
    copy.wait()


def chunk_of(rows, at):
    blocks = CHUNK // CAP
    return rows[pl.ds(at * blocks, blocks)].reshape(CHUNK, rows.shape[2])


def forward_kernel(tiles, source, gate_w, up_w, down_w, out, rows, hidden, semaphore):
    step = pl.program_id(0)

    @pl.when(step == 0)
    def _():
        load(source, 0, rows, semaphore)

    for index in range(tiles):

        @pl.when(step == index)
        def _():
            @pl.loop(0, hidden.shape[0] // CHUNK)
            def _(at):
                span = pl.ds(pl.multiple_of(at * CHUNK, CHUNK), CHUNK)
                values = chunk_of(rows, at)
                gate = jnp.dot(values, gate_w[...], preferred_element_type=f32)
                up = jnp.dot(values, up_w[...], preferred_element_type=f32)
                size = gate_w.shape[1]
                value = gate / (1.0 + jnp.exp(-gate)) * up
                hidden[span, index * size : (index + 1) * size] = value.astype(bf16)

    @pl.when(step >= tiles)
    def _():
        out[...] = jnp.dot(hidden[...], down_w[...], preferred_element_type=f32).astype(bf16)


def expert_forward(source, gate_w, up_w, down_w):
    width, hid = gate_w.shape
    total = source.shape[0] * CAP
    tile, out_tile = 256, 1024
    tiles, out_tiles = hid // tile, width // out_tile
    project = pl.BlockSpec((width, tile), lambda i: (0, jnp.minimum(i, tiles - 1)))
    late = lambda i: (0, jnp.maximum(i - tiles, 0))
    return pl.pallas_call(
        functools.partial(forward_kernel, tiles),
        grid=(tiles + out_tiles,),
        in_specs=[ANY, project, project, pl.BlockSpec((hid, out_tile), late)],
        out_specs=pl.BlockSpec((total, out_tile), late),
        out_shape=jax.ShapeDtypeStruct((total, width), bf16),
        scratch_shapes=[
            pltpu.VMEM((source.shape[0], CAP, width), bf16),
            pltpu.VMEM((total, hid), bf16),
            pltpu.SemaphoreType.DMA,
        ],
        compiler_params=params(1),
        cost_estimate=cost(6 * total * width * hid, 6 * width * hid + 4 * total * width),
    )(source, gate_w, up_w, down_w)


def hidden_grad_kernel(source, down_w, out, rows, semaphore):
    @pl.when(pl.program_id(0) == 0)
    def _():
        load(source, CAP, rows, semaphore)

    @pl.loop(0, out.shape[0] // CHUNK)
    def _(at):
        span = pl.ds(pl.multiple_of(at * CHUNK, CHUNK), CHUNK)
        out[span, :] = lax.dot_general(
            chunk_of(rows, at), down_w[...], (((1,), (1,)), ((), ())), preferred_element_type=f32
        )


def expert_hidden_grad(source, down_w):
    hid, width = down_w.shape
    total = source.shape[0] * CAP
    tile = 256
    return pl.pallas_call(
        hidden_grad_kernel,
        grid=(hid // tile,),
        in_specs=[ANY, pl.BlockSpec((tile, width), lambda i: (i, 0))],
        out_specs=pl.BlockSpec((total, tile), lambda i: (0, i)),
        out_shape=jax.ShapeDtypeStruct((total, hid), f32),
        scratch_shapes=[pltpu.VMEM((source.shape[0], CAP, width), bf16), pltpu.SemaphoreType.DMA],
        compiler_params=params(1),
        cost_estimate=cost(2 * total * width * hid, 2 * width * hid + 2 * total * width),
    )(source, down_w)


def gate_grads_kernel(source, gate_w, up_w, hidden_ref, gate_out, up_out, rows, semaphore):
    @pl.when(pl.program_id(0) == 0)
    def _():
        load(source, 0, rows, semaphore)

    @pl.loop(0, gate_out.shape[0] // CHUNK)
    def _(at):
        span = pl.ds(pl.multiple_of(at * CHUNK, CHUNK), CHUNK)
        values = chunk_of(rows, at)
        gate = jnp.dot(values, gate_w[...], preferred_element_type=f32)
        up = jnp.dot(values, up_w[...], preferred_element_type=f32)
        hidden_grad = hidden_ref[span, :]
        sig = 1.0 / (1.0 + jnp.exp(-gate))
        gate_out[span, :] = (hidden_grad * up * sig * (1.0 + gate * (1.0 - sig))).astype(bf16)
        up_out[span, :] = (hidden_grad * gate * sig).astype(bf16)


def expert_gate_grads(source, gate_w, up_w, hidden_grad):
    width, hid = gate_w.shape
    total = source.shape[0] * CAP
    tile = 256
    project = pl.BlockSpec((width, tile), lambda i: (0, i))
    column = pl.BlockSpec((total, tile), lambda i: (0, i))
    return pl.pallas_call(
        gate_grads_kernel,
        grid=(hid // tile,),
        in_specs=[ANY, project, project, column],
        out_specs=[column, column],
        out_shape=[jax.ShapeDtypeStruct((total, hid), bf16)] * 2,
        scratch_shapes=[pltpu.VMEM((source.shape[0], CAP, width), bf16), pltpu.SemaphoreType.DMA],
        compiler_params=params(1),
        cost_estimate=cost(4 * total * width * hid, 4 * width * hid + 2 * total * width + 8 * total * hid),
    )(source, gate_w, up_w, hidden_grad)


def entry_grads_kernel(gate_grad, up_grad, gate_w, up_w, out):
    contract = (((1,), (1,)), ((), ()))

    @pl.loop(0, gate_grad.shape[0] // CHUNK)
    def _(at):
        span = pl.ds(pl.multiple_of(at * CHUNK, CHUNK), CHUNK)
        rows = lax.dot_general(gate_grad[span, :], gate_w[...], contract, preferred_element_type=f32)
        rows = rows + lax.dot_general(up_grad[span, :], up_w[...], contract, preferred_element_type=f32)
        out[span, :] = rows.astype(bf16)


def expert_entry_grads(gate_grad, up_grad, gate_w, up_w, part, parts):
    total, hid = gate_grad.shape
    width = gate_w.shape[0] // parts
    tile = 512
    steps = width // tile
    weights = pl.BlockSpec((tile, hid), lambda i: (part * steps + i, 0))
    return pl.pallas_call(
        entry_grads_kernel,
        grid=(steps,),
        in_specs=[whole(gate_grad.shape), whole(up_grad.shape), weights, weights],
        out_specs=pl.BlockSpec((total, tile), lambda i: (0, i)),
        out_shape=jax.ShapeDtypeStruct((total, width), bf16),
        compiler_params=params(1),
        cost_estimate=cost(4 * total * width * hid, 4 * width * hid + 2 * total * width + 4 * total * hid),
    )(gate_grad, up_grad, gate_w, up_w)


def exchange(pieces):
    return lax.all_to_all(pieces, "expert", split_axis=0, concat_axis=0, tiled=True)


def from_slots(place, table):
    return lax.dot_general(place, table, (((0,), (0,)), ((), ())), preferred_element_type=f32)


def on_device(
    onward_block_activation,
    reverse_stored_activation,
    reverse_result_derivative,
    onward_specialist_choices,
    reverse_specialist_choices,
    onward_mixing_coefficients,
    reverse_mixing_coefficients,
    quota_table,
    rescaling_factor_list,
    gating_projection_matrix,
    expansion_matrix,
    contraction_matrix,
):
    scaling = rescaling_factor_list[0]
    gate_w = gating_projection_matrix[0, 0]
    up_w = expansion_matrix[0, 0]
    down_w = contraction_matrix[0, 0]
    quota = quota_table[0]
    count, width = quota.shape[0], gate_w.shape[0]
    input_f, input_b, grad_y = onward_block_activation[0], reverse_stored_activation[0], reverse_result_derivative[0]
    weight_f, weight_b = onward_mixing_coefficients[0].T, reverse_mixing_coefficients[0].T
    slots_f = slots_of(onward_specialist_choices[0].T, quota)
    slots_b = slots_of(reverse_specialist_choices[0].T, quota)
    values_f, values_b = input_f.astype(f32), input_b.astype(f32)
    inverse_f, inverse_b = inverse_rms(values_f), inverse_rms(values_b)

    send_f = dispatch(count, slots_f, weight_f, inverse_f, scaling[None], input_f, None)
    send_b = dispatch(count, slots_b, weight_b, inverse_b, scaling[None], input_b, grad_y)
    rows_f = exchange(send_f)
    rows_b = exchange(after(send_b, rows_f))

    out_f = expert_forward(rows_f, gate_w, up_w, down_w)
    table_f = exchange(after(out_f, rows_b).reshape(count, CAP, width)).reshape(count * CAP, width)

    hidden_grad = expert_hidden_grad(rows_b, down_w)
    gate_grad, up_grad = expert_gate_grads(rows_b, gate_w, up_w, hidden_grad)
    out_b = expert_entry_grads(gate_grad, up_grad, gate_w, up_w, 0, 1)
    table_b = exchange(after(out_b, table_f).reshape(count, CAP, width)).reshape(count * CAP, width)

    first, second = masks(slots_f, count * CAP)
    mixed = jnp.where(first, weight_f[0:1, :], 0.0) + jnp.where(second, weight_f[1:2, :], 0.0)
    high = mixed.astype(bf16)
    low = (mixed - high.astype(f32)).astype(bf16)
    fwd = values_f + from_slots(high, table_f) + from_slots(low, table_f)
    fwd_next = passed_along(fwd.astype(bf16), "pipe", 1)

    first, second = masks(slots_b, count * CAP)
    scaled = scaling * from_slots((first | second).astype(bf16), table_b)
    inner = jnp.mean(values_b * scaled, axis=-1, keepdims=True)
    grad = grad_y.astype(f32) + inverse_b * scaled
    grad = grad - values_b * (inverse_b * inverse_b * inverse_b * inner)
    grad_next = passed_along(grad.astype(bf16), "pipe", -1)
    return (fwd_next[None], grad_next[None])


def solution(mesh):
    blocks = P("pipe", "expert", None)
    in_specs = (blocks,) * 7 + (P("pipe", None),) * 2 + (P("pipe", "expert", None, None),) * 3
    return jax.shard_map(
        on_device, mesh=mesh, in_specs=in_specs, out_specs=(blocks, blocks), check_vma=False
    )
```

time: 320 us -> 314 us (0.981)
  matrix products: 86.5 us -> 10.3 us
  Pallas kernels: 0 us -> 68.8 us
  starting transfers between devices: 33.3 us -> 28.5 us
    dot_general x12 -> x2, matrix products: 77.2 us -> 0.95 us  [slots_of(): jnp.dot(named, (row < column).astype(bf16), preferred_element_type=f32)]
    pallas_call x0 -> x6, Pallas kernels: none -> 68.8 us  [the longest x1 19.5 us: expert_forward(): pl.pallas_call(functools.partial(forward_kernel, tiles), grid=(tiles + ou...]
    all_to_all x5 -> x4, starting transfers between devices: 24.6 us -> 19.7 us  [exchange(): lax.all_to_all(pieces, 'expert', split_axis=0, concat_axis=0, tiled=True)]
    all_to_all x5 -> x4, waiting for transfers between devices: 171 us -> 173 us  [exchange(): lax.all_to_all(pieces, 'expert', split_axis=0, concat_axis=0, tiled=True)]
  transfers between devices with their start and end apart: 7 -> 6, of which waited for: 7 -> 6; matrix products, arithmetic and copies ran while one was open for 26% -> 4% of each run, Pallas kernels for 0% -> 20%
where the time goes in v2:
time: 314 us; the launch traced here: 313 us
  waiting for transfers between devices  195 us (62%)
  Pallas kernels  68.8 us (22%)
  starting transfers between devices  28.5 us (9%)
  matrix products  10.3 us (3%)
  local copies, waits for them, and re-layouts  4.99 us (2%)
  other arithmetic  4.37 us (1%)
    all_to_all x4, waiting for transfers between devices, exchange(): lax.all_to_all(pieces, 'expert', split_axis=0, concat_axis=0, tiled=True)  173 us
    ppermute x2, waiting for transfers between devices, passed_along(): return lax.ppermute(value, axis, pairs)  21.8 us
    all_to_all x4, starting transfers between devices, exchange(): lax.all_to_all(pieces, 'expert', split_axis=0, concat_axis=0, tiled=True)  19.7 us
    pallas_call x1, Pallas kernels, expert_forward(): pl.pallas_call(functools.partial(forward_kernel, tiles), grid=(tiles + ou...  19.5 us
    pallas_call x1, Pallas kernels, expert_gate_grads(): pl.pallas_call(gate_grads_kernel, grid=(hid // tile,), in_specs=[ANY, pro...  14 us
    pallas_call x1, Pallas kernels, expert_entry_grads(): pl.pallas_call(entry_grads_kernel, grid=(steps,), in_specs=[whole(gate_gr...  13.7 us
    pallas_call x2, Pallas kernels, dispatch(): pl.pallas_call(dispatch_kernel, grid=(width // tile,), in_specs=[whole(pl...  12.1 us
    pallas_call x1, Pallas kernels, expert_hidden_grad(): pl.pallas_call(hidden_grad_kernel, grid=(hid // tile,), in_specs=[ANY, pl...  9.53 us
  transfers between devices with their start and end apart: 6, of which 6 were waited for; matrix products, arithmetic and copies ran while one was open for 4% of the time, Pallas kernels for 20%

profile of v2, /device:TPU:0, one launch (start us, length us, event | category | flops | bytes accessed | tf_op | source)
XLA Modules:
  0.0 312.6 jit_solution(15900130153948994367)
XLA Ops:
  0.6 0.8 slice_bitcast_fusion.2
  1.4 0.8 slice_bitcast_fusion.5
  2.1 1.5 fusion.1
  3.7 0.8 copy.14.inverse_ref
  4.4 0.1 convolution_convert_fusion
  4.6 0.8 select_reduce_fusion.7
  5.4 0.8 compare_select_fusion.1
  6.1 0.6 pad_add_fusion.place_ref
  6.7 5.3 %shard_map.131 = bf16[16,32,4096]{2,1,0:T(8,128)(2,1)} custom-call(s32[2,128]{1,0:T(2,128)} %pad_add_fusion.place_ref, f32[2,128]{1,0:T(2,128)} %bitcast.100, f32[128,1]{1,0:T(8,128)} %copy.14.inverse_ref, f32[1,4096]{1,0:T(1,128)} %scaling_ref.3, bf16[128,4096]{1,0:T(8,128)(2,1)} %bitcast.83, bf16[128,4096]{1,0:T(8,128)(2,1)} %bitcast.84), custom_call_target="tpu_custom_call" | custom-call | flops 536870912 | bytes 6291456 | tf_op jit(solution)/shard_map/pallas_call | solution.py:95
  12.0 0.0 copy-start.1
  12.0 5.8 %all-to-all-start = ((bf16[16,32,4096]{2,1,0:T(8,128)(2,1)}), bf16[16,32,4096]{2,1,0:T(8,128)(2,1)}, u32[]{:S(2)}, u32[]{:S(2)}) async-start(bf16[16,32,4096]{2,1,0:T(8,128)(2,1)} %shard_map.131), calls=%async_computation | async-start | bytes 8388608 | tf_op jit(solution)/shard_map/all_to_all | solution.py:269
  17.8 0.0 copy-done.1
  17.8 0.3 fusion.2
  18.1 0.8 copy.15.inverse_ref
  18.8 0.6 pad_add_fusion.1.place_ref
  19.4 6.8 %shard_map.133 = bf16[16,64,4096]{2,1,0:T(8,128)(2,1)} custom-call(s32[2,128]{1,0:T(2,128)} %pad_add_fusion.1.place_ref, f32[2,128]{1,0:T(2,128)} %bitcast.106, f32[128,1]{1,0:T(8,128)} %copy.15.inverse_ref, f32[1,4096]{1,0:T(1,128)} %scaling_ref.3, bf16[128,4096]{1,0:T(8,128)(2,1)} %bitcast.85, bf16[128,4096]{1,0:T(8,128)(2,1)} %bitcast.90), custom_call_target="tpu_custom_call" | custom-call | flops 1073741824 | bytes 10485760 | tf_op jit(solution)/shard_map/pallas_call | solution.py:95
  26.2 42.0 %all-to-all-done.source = bf16[16,32,4096]{2,1,0:T(8,128)(2,1)} async-done(((bf16[16,32,4096]{2,1,0:T(8,128)(2,1)}), bf16[16,32,4096]{2,1,0:T(8,128)(2,1)}, u32[]{:S(2)}, u32[]{:S(2)}) %all-to-all-start) | async-done | bytes 4194336 | tf_op jit(solution)/shard_map/all_to_all | solution.py:269
  68.2 4.7 %all-to-all-start.1 = ((bf16[16,64,4096]{2,1,0:T(8,128)(2,1)}), bf16[16,64,4096]{2,1,0:T(8,128)(2,1)}, u32[]{:S(2)}, u32[]{:S(2)}) async-start(bf16[16,64,4096]{2,1,0:T(8,128)(2,1)} %shard_map.133), calls=%async_computation.1 | async-start | bytes 16777216 | tf_op jit(solution)/shard_map/all_to_all | solution.py:269
  72.9 19.5 %shard_map.132 = bf16[512,4096]{1,0:T(8,128)(2,1)} custom-call(bf16[16,32,4096]{2,1,0:T(8,128)(2,1)} %all-to-all-done.source, bf16[4096,768]{1,0:T(8,128)(2,1)} %bitcast.107, bf16[4096,768]{1,0:T(8,128)(2,1)} %bitcast.110, bf16[768,4096]{1,0:T(8,128)(2,1)} %bitcast.86), custom_call_target="tpu_custom_call" | custom-call | flops 9663676416 | bytes 27262976 | tf_op jit(solution)/shard_map/pallas_call | solution.py:160
  92.4 75.8 %all-to-all-done.1.source = bf16[16,64,4096]{2,1,0:T(8,128)(2,1)} async-done(((bf16[16,64,4096]{2,1,0:T(8,128)(2,1)}), bf16[16,64,4096]{2,1,0:T(8,128)(2,1)}, u32[]{:S(2)}, u32[]{:S(2)}) %all-to-all-start.1) | async-done | bytes 8388640 | tf_op jit(solution)/shard_map/all_to_all | solution.py:269
  168.2 4.5 %all-to-all-start.2 = ((bf16[16,32,4096]{2,1,0:T(8,128)(2,1)}), bf16[16,32,4096]{2,1,0:T(8,128)(2,1)}, u32[]{:S(2)}, u32[]{:S(2)}) async-start(bf16[16,32,4096]{2,1,0:T(8,128)(2,1)} %bitcast.89), calls=%async_computation.2 | async-start | bytes 8388608 | tf_op jit(solution)/shard_map/all_to_all | solution.py:269
  172.8 9.5 %shard_map.134.hidden_ref = f32[512,768]{1,0:T(8,128)} custom-call(bf16[16,64,4096]{2,1,0:T(8,128)(2,1)} %all-to-all-done.1.source, bf16[768,4096]{1,0:T(8,128)(2,1)} %bitcast.87), custom_call_target="tpu_custom_call" | custom-call | flops 3221225472 | bytes 10485760 | tf_op jit(solution)/shard_map/pallas_call | solution.py:193
  182.3 14.0 %shard_map.135 = (bf16[512,768]{1,0:T(8,128)(2,1)}, bf16[512,768]{1,0:T(8,128)(2,1)}) custom-call(bf16[16,64,4096]{2,1,0:T(8,128)(2,1)} %all-to-all-done.1.source, bf16[4096,768]{1,0:T(8,128)(2,1)} %bitcast.108, bf16[4096,768]{1,0:T(8,128)(2,1)} %bitcast.111, f32[512,768]{1,0:T(8,128)} %shard_map.134.hidden_ref), custom_call_target="tpu_custom_call" | custom-call | flops 6442450944 | bytes 19922944 | tf_op jit(solution)/shard_map/pallas_call | solution.py:228
  196.4 13.7 %shard_map.136 = bf16[512,4096]{1,0:T(8,128)(2,1)} custom-call(bf16[512,768]{1,0:T(8,128)(2,1)} %get-tuple-element.9.gate_grad, bf16[512,768]{1,0:T(8,128)(2,1)} %get-tuple-element.10.up_grad, bf16[4096,768]{1,0:T(8,128)(2,1)} %bitcast.109, bf16[4096,768]{1,0:T(8,128)(2,1)} %bitcast.112), custom_call_target="tpu_custom_call" | custom-call | flops 6442450944 | bytes 18350080 | tf_op jit(solution)/shard_map/pallas_call | solution.py:257
  210.0 13.1 %all-to-all-done.2 = bf16[16,32,4096]{2,1,0:T(8,128)(2,1)} async-done(((bf16[16,32,4096]{2,1,0:T(8,128)(2,1)}), bf16[16,32,4096]{2,1,0:T(8,128)(2,1)}, u32[]{:S(2)}, u32[]{:S(2)}) %all-to-all-start.2) | async-done | bytes 4194336 | tf_op jit(solution)/shard_map/all_to_all | solution.py:269
  223.2 0.0 copy-start.5
  223.2 0.0 copy-start
  223.2 4.7 %all-to-all-start.3 = ((bf16[16,32,4096]{2,1,0:T(8,128)(2,1)}), bf16[16,32,4096]{2,1,0:T(8,128)(2,1)}, u32[]{:S(2)}, u32[]{:S(2)}) async-start(bf16[16,32,4096]{2,1,0:T(8,128)(2,1)} %bitcast.88), calls=%async_computation.3 | async-start | bytes 8388608 | tf_op jit(solution)/shard_map/all_to_all | solution.py:269
  227.8 0.0 copy-done.5
  227.9 0.0 copy-done
  227.9 3.0 convolution_add_fusion.1
  230.8 0.0 copy-start.2
  230.8 0.0 copy-start.4
  230.9 3.1 fusion
  234.0 2.0 collective-permute-start
  236.0 42.2 %all-to-all-done.3 = bf16[16,32,4096]{2,1,0:T(8,128)(2,1)} async-done(((bf16[16,32,4096]{2,1,0:T(8,128)(2,1)}), bf16[16,32,4096]{2,1,0:T(8,128)(2,1)}, u32[]{:S(2)}, u32[]{:S(2)}) %all-to-all-start.3) | async-done | bytes 4194336 | tf_op jit(solution)/shard_map/all_to_all | solution.py:269
  278.2 0.0 copy-done.2
  278.2 0.0 copy-done.4
  278.2 0.0 copy-start.3
  278.2 3.3 %fusion.3 = (f32[128]{0:T(128)S(1)}, f32[128,4096]{1,0:T(8,128)S(1)}) fusion(bf16[1,128,4096]{2,1,0:T(8,128)(2,1)S(1)} %copy-done.2, bf16[512,4096]{1,0:T(8,128)(2,1)} %bitcast.43, s32[128]{0:T(128)S(1)} %bitcast.99, s32[128]{0:T(128)S(1)} %bitcast.98, f32[4096]{0:T(1024)S(1)} %bitcast.93), kind=kOutput, calls=%fused_computation.10 | convolution fusion | flops 539164544 | bytes 7357952 | tf_op jit(solution)/shard_map/dot_general | solution.py:273
  281.5 0.0 copy-done.3
  281.5 0.6 fusion.5
  282.2 6.7 %collective-permute-start.1 = (bf16[128,4096]{1,0:T(8,128)(2,1)S(1)}, bf16[128,4096]{1,0:T(8,128)(2,1)S(1)}, u32[]{:S(2)}, u32[]{:S(2)}) collective-permute-start(bf16[128,4096]{1,0:T(8,128)(2,1)S(1)} %fusion.5), channel_id=1, source_target_pairs={{0,112},{16,0},{32,16},{48,32},{64,48},{80,64},{96,80},{112,96},{1... | collective-permute-start | bytes 3145736 | tf_op jit(solution)/shard_map/ppermute | solution.py:34
  288.9 15.2 %collective-permute-done = bf16[128,4096]{1,0:T(8,128)(2,1)S(1)} collective-permute-done((bf16[128,4096]{1,0:T(8,128)(2,1)S(1)}, bf16[128,4096]{1,0:T(8,128)(2,1)S(1)}, u32[]{:S(2)}, u32[]{:S(2)}) %collective-permute-start) | collective-permute-done | bytes 1048608 | tf_op jit(solution)/shard_map/ppermute | solution.py:34
  304.1 6.5 %collective-permute-done.1 = bf16[128,4096]{1,0:T(8,128)(2,1)S(1)} collective-permute-done((bf16[128,4096]{1,0:T(8,128)(2,1)S(1)}, bf16[128,4096]{1,0:T(8,128)(2,1)S(1)}, u32[]{:S(2)}, u32[]{:S(2)}) %collective-permute-start.1) | collective-permute-done | bytes 1048608 | tf_op jit(solution)/shard_map/ppermute | solution.py:34
  310.7 1.0 copy.18
  311.6 1.0 copy.19
  (4 shorter events, 0.0 us)
Async XLA Ops:
  12.0 5.8 %copy-start.1 = (bf16[1,128,4096]{2,1,0:T(8,128)(2,1)S(1)}, bf16[1,128,4096]{2,1,0:T(8,128)(2,1)}, u32[]{:S(2)}) copy-start(bf16[1,128,4096]{2,1,0:T(8,128)(2,1)} %param.13) | copy-start | bytes 3145732
  12.0 56.2 %all-to-all-start = ((bf16[16,32,4096]{2,1,0:T(8,128)(2,1)}), bf16[16,32,4096]{2,1,0:T(8,128)(2,1)}, u32[]{:S(2)}, u32[]{:S(2)}) async-start(bf16[16,32,4096]{2,1,0:T(8,128)(2,1)} %shard_map.131), calls=%async_computation | async-start | bytes 8388608 | tf_op jit(solution)/shard_map/all_to_all | solution.py:269
  68.2 100.1 %all-to-all-start.1 = ((bf16[16,64,4096]{2,1,0:T(8,128)(2,1)}), bf16[16,64,4096]{2,1,0:T(8,128)(2,1)}, u32[]{:S(2)}, u32[]{:S(2)}) async-start(bf16[16,64,4096]{2,1,0:T(8,128)(2,1)} %shard_map.133), calls=%async_computation.1 | async-start | bytes 16777216 | tf_op jit(solution)/shard_map/all_to_all | solution.py:269
  168.2 54.9 %all-to-all-start.2 = ((bf16[16,32,4096]{2,1,0:T(8,128)(2,1)}), bf16[16,32,4096]{2,1,0:T(8,128)(2,1)}, u32[]{:S(2)}, u32[]{:S(2)}) async-start(bf16[16,32,4096]{2,1,0:T(8,128)(2,1)} %bitcast.89), calls=%async_computation.2 | async-start | bytes 8388608 | tf_op jit(solution)/shard_map/all_to_all | solution.py:269
  223.2 4.7 %copy-start.5 = (f32[1,128,2]{1,2,0:T(2,128)S(1)}, f32[1,128,2]{1,2,0:T(2,128)}, u32[]{:S(2)}) copy-start(f32[1,128,2]{1,2,0:T(2,128)} %param.17) | copy-start | bytes 3076
  223.2 4.7 %copy-start = (bf16[1,128,4096]{2,1,0:T(8,128)(2,1)S(1)}, bf16[1,128,4096]{2,1,0:T(8,128)(2,1)}, u32[]{:S(2)}) copy-start(bf16[1,128,4096]{2,1,0:T(8,128)(2,1)} %param.12) | copy-start | bytes 3145732
  223.2 55.0 %all-to-all-start.3 = ((bf16[16,32,4096]{2,1,0:T(8,128)(2,1)}), bf16[16,32,4096]{2,1,0:T(8,128)(2,1)}, u32[]{:S(2)}, u32[]{:S(2)}) async-start(bf16[16,32,4096]{2,1,0:T(8,128)(2,1)} %bitcast.88), calls=%async_computation.3 | async-start | bytes 8388608 | tf_op jit(solution)/shard_map/all_to_all | solution.py:269
  230.8 47.4 %copy-start.2 = (bf16[1,128,4096]{2,1,0:T(8,128)(2,1)S(1)}, bf16[1,128,4096]{2,1,0:T(8,128)(2,1)}, u32[]{:S(2)}) copy-start(bf16[1,128,4096]{2,1,0:T(8,128)(2,1)} %param.13) | copy-start | bytes 3145732
  230.8 47.4 %copy-start.4 = (f32[1,4096]{1,0:T(1,128)S(1)}, f32[1,4096]{1,0:T(1,128)}, u32[]{:S(2)}) copy-start(f32[1,4096]{1,0:T(1,128)} %scaling_ref.3) | copy-start | bytes 49156
  234.0 70.2 %collective-permute-start = (bf16[128,4096]{1,0:T(8,128)(2,1)S(1)}, bf16[128,4096]{1,0:T(8,128)(2,1)S(1)}, u32[]{:S(2)}, u32[]{:S(2)}) collective-permute-start(bf16[128,4096]{1,0:T(8,128)(2,1)S(1)} %fusion), channel_id=1, source_target_pairs={{0,16},{16,32},{32,48},{48,64},{64,80},{80,96},{96,112},{112,0},{1... | collective-permute-start | bytes 3145736 | tf_op jit(solution)/shard_map/ppermute | solution.py:34
  278.2 3.3 %copy-start.3 = (bf16[1,128,4096]{2,1,0:T(8,128)(2,1)S(1)}, bf16[1,128,4096]{2,1,0:T(8,128)(2,1)}, u32[]{:S(2)}) copy-start(bf16[1,128,4096]{2,1,0:T(8,128)(2,1)} %param.14) | copy-start | bytes 3145732
  282.2 28.5 %collective-permute-start.1 = (bf16[128,4096]{1,0:T(8,128)(2,1)S(1)}, bf16[128,4096]{1,0:T(8,128)(2,1)S(1)}, u32[]{:S(2)}, u32[]{:S(2)}) collective-permute-start(bf16[128,4096]{1,0:T(8,128)(2,1)S(1)} %fusion.5), channel_id=1, source_target_pairs={{0,112},{16,0},{32,16},{48,32},{64,48},{80,64},{96,80},{112,96},{1... | collective-permute-start | bytes 3145736 | tf_op jit(solution)/shard_map/ppermute | solution.py:34

commit v3 on v2

--- a/solution.py
+++ b/solution.py
@@ -34,37 +34,8 @@
     return lax.ppermute(value, axis, pairs)
 
 
-def inverse_rms(values):
-    return lax.rsqrt(jnp.mean(values * values, axis=-1, keepdims=True) + EPSILON)
-
-
 def after(value, *others):
     return lax.optimization_barrier((value, *others))[0]
-
-
-def slots_of(chosen, quota):
-    count, tokens = quota.shape[0], chosen.shape[1]
-    experts = lax.broadcasted_iota(jnp.int32, (count, tokens), 0)
-    first = experts == chosen[0][None, :]
-    second = experts == chosen[1][None, :]
-    named = first.astype(bf16) + second.astype(bf16)
-    row = lax.broadcasted_iota(jnp.int32, (tokens, tokens), 0)
-    column = lax.broadcasted_iota(jnp.int32, (tokens, tokens), 1)
-    before = jnp.dot(
-        named, (row < column).astype(bf16), preferred_element_type=f32
-    ).astype(jnp.int32)
-
-    def slot(mask, ranks, ids):
-        rank = jnp.sum(jnp.where(mask, ranks, 0), axis=0)
-        limit = jnp.sum(jnp.where(mask, quota[:, None], 0), axis=0)
-        return jnp.where(rank < limit, ids * CAP + rank, -1)
-
-    return jnp.stack(
-        [
-            slot(first, before, chosen[0]),
-            slot(second, before + first.astype(jnp.int32), chosen[1]),
-        ]
-    )
 
 
 def masks(place, count):
@@ -72,14 +43,45 @@
     return rows == place[0:1, :], rows == place[1:2, :]
 
 
-def dispatch_kernel(place_ref, weight_ref, inverse_ref, scaling_ref, values_ref, grad_ref, out):
-    count, rows_each, tile = out.shape
+def slots_of(chosen, quota, count):
+    tokens = chosen.shape[1]
+    first, second = masks(chosen, count)
+    first, second = jnp.where(first, 1.0, 0.0), jnp.where(second, 1.0, 0.0)
+    row = lax.broadcasted_iota(jnp.int32, (tokens, tokens), 0)
+    column = lax.broadcasted_iota(jnp.int32, (tokens, tokens), 1)
+    earlier = jnp.where(row < column, 1.0, 0.0).astype(bf16)
+    before = jnp.dot((first + second).astype(bf16), earlier, preferred_element_type=f32)
+    slots = []
+    for at, (mask, ranks) in enumerate(((first, before), (second, before + first))):
+        ids = chosen[at : at + 1, :]
+        rank = jnp.sum(mask * ranks, axis=0, keepdims=True).astype(jnp.int32)
+        limit = jnp.zeros_like(ids)
+        for expert in range(count):
+            limit = jnp.where(ids == expert, quota[0, expert], limit)
+        slots.append(jnp.where(rank < limit, ids * CAP + rank, -1))
+    return slots
+
+
+def dispatch_kernel(has_grad, quota, chosen_ref, weight_ref, scaling_ref, values_ref, *refs):
+    grad_ref, (out, place_ref, inverse_ref) = refs[0], refs[-3:]
+    count, _, tile = out.shape
+    step = pl.program_id(0)
+
+    @pl.when(step == 0)
+    def _():
+        values = values_ref[...].astype(f32)
+        inverse_ref[...] = lax.rsqrt(jnp.mean(values * values, axis=1, keepdims=True) + EPSILON)
+        first, second = slots_of(chosen_ref[...], quota, count)
+        place_ref[0:1, :] = first
+        place_ref[1:2, :] = second
+
     first, second = masks(place_ref[...], count * CAP)
     chosen = jnp.where(first | second, 1.0, 0.0).astype(bf16)
-    normed = values_ref[...].astype(f32) * inverse_ref[...] * scaling_ref[...]
-    rows = jnp.dot(chosen, normed.astype(bf16), preferred_element_type=f32)
+    values = values_ref[:, pl.ds(pl.multiple_of(step * tile, tile), tile)].astype(f32)
+    normed = (values * inverse_ref[...] * scaling_ref[...]).astype(bf16)
+    rows = jnp.dot(chosen, normed, preferred_element_type=f32)
     out[:, :CAP, :] = rows.astype(bf16).reshape(count, CAP, tile)
-    if rows_each > CAP:
+    if has_grad:
         weight = weight_ref[...]
         scale = jnp.where(first, weight[0:1, :], 0.0) + jnp.where(second, weight[1:2, :], 0.0)
         rows = jnp.dot(chosen, grad_ref[...], preferred_element_type=f32)
@@ -87,27 +89,35 @@
         out[:, CAP:, :] = rows.astype(bf16).reshape(count, CAP, tile)
 
 
-def dispatch(count, place, weight, inverse, scaling, values, grad):
-    tokens, width = values.shape
+def dispatch(quota, chosen, weight, scaling, values, grad=None):
+    count, (tokens, width) = quota.shape[1], values.shape
     tile = 1024
     rows_each = CAP if grad is None else 2 * CAP
     column = pl.BlockSpec((tokens, tile), lambda i: (0, i))
     return pl.pallas_call(
-        dispatch_kernel,
+        functools.partial(dispatch_kernel, grad is not None),
         grid=(width // tile,),
         in_specs=[
-            whole(place.shape),
+            pl.BlockSpec(memory_space=pltpu.SMEM),
+            whole(chosen.shape),
             whole(weight.shape),
-            whole(inverse.shape),
             pl.BlockSpec((1, tile), lambda i: (0, i)),
-            column,
-            column,
+            whole(values.shape),
+        ]
+        + [column] * (grad is not None),
+        out_specs=[
+            pl.BlockSpec((count, rows_each, tile), lambda i: (0, 0, i)),
+            whole(chosen.shape),
+            whole((tokens, 1)),
         ],
-        out_specs=pl.BlockSpec((count, rows_each, tile), lambda i: (0, 0, i)),
-        out_shape=jax.ShapeDtypeStruct((count, rows_each, width), bf16),
+        out_shape=[
+            jax.ShapeDtypeStruct((count, rows_each, width), bf16),
+            jax.ShapeDtypeStruct(chosen.shape, jnp.int32),
+            jax.ShapeDtypeStruct((tokens, 1), f32),
+        ],
         compiler_params=params(1),
         cost_estimate=cost(2 * count * rows_each * tokens * width, 2 * (count * rows_each + 2 * tokens) * width),
-    )(place, weight, inverse, scaling, values, values if grad is None else grad)
+    )(quota, chosen, weight, scaling, values, *([] if grad is None else [grad]))
 
 
 CHUNK = 256
@@ -271,6 +281,23 @@
 
 def from_slots(place, table):
     return lax.dot_general(place, table, (((0,), (0,)), ((), ())), preferred_element_type=f32)
+
+
+def written_kernel(source, out):
+    out[...] = source[...]
+
+
+def written(rows):
+    block = pl.BlockSpec((rows.shape[0] // 2, rows.shape[1]), lambda i: (i, 0))
+    return pl.pallas_call(
+        written_kernel,
+        grid=(2,),
+        in_specs=[block],
+        out_specs=block,
+        out_shape=jax.ShapeDtypeStruct(rows.shape, rows.dtype),
+        compiler_params=params(1),
+        cost_estimate=cost(0, 4 * rows.size),
+    )(rows)
 
 
 def on_device(
@@ -287,27 +314,22 @@
     expansion_matrix,
     contraction_matrix,
 ):
-    scaling = rescaling_factor_list[0]
+    scaling = rescaling_factor_list
     gate_w = gating_projection_matrix[0, 0]
     up_w = expansion_matrix[0, 0]
     down_w = contraction_matrix[0, 0]
-    quota = quota_table[0]
-    count, width = quota.shape[0], gate_w.shape[0]
+    count, width = quota_table.shape[1], gate_w.shape[0]
     input_f, input_b, grad_y = onward_block_activation[0], reverse_stored_activation[0], reverse_result_derivative[0]
     weight_f, weight_b = onward_mixing_coefficients[0].T, reverse_mixing_coefficients[0].T
-    slots_f = slots_of(onward_specialist_choices[0].T, quota)
-    slots_b = slots_of(reverse_specialist_choices[0].T, quota)
-    values_f, values_b = input_f.astype(f32), input_b.astype(f32)
-    inverse_f, inverse_b = inverse_rms(values_f), inverse_rms(values_b)
-
-    send_f = dispatch(count, slots_f, weight_f, inverse_f, scaling[None], input_f, None)
-    send_b = dispatch(count, slots_b, weight_b, inverse_b, scaling[None], input_b, grad_y)
+    chosen_f, chosen_b = onward_specialist_choices[0].T, reverse_specialist_choices[0].T
+
+    send_f, slots_f, _ = dispatch(quota_table, chosen_f, weight_f, scaling, input_f)
     rows_f = exchange(send_f)
+    send_b, slots_b, inverse_b = dispatch(quota_table, chosen_b, weight_b, scaling, input_b, grad_y)
     rows_b = exchange(after(send_b, rows_f))
 
     out_f = expert_forward(rows_f, gate_w, up_w, down_w)
     table_f = exchange(after(out_f, rows_b).reshape(count, CAP, width)).reshape(count * CAP, width)
-
     hidden_grad = expert_hidden_grad(rows_b, down_w)
     gate_grad, up_grad = expert_gate_grads(rows_b, gate_w, up_w, hidden_grad)
     out_b = expert_entry_grads(gate_grad, up_grad, gate_w, up_w, 0, 1)
@@ -317,16 +339,17 @@
     mixed = jnp.where(first, weight_f[0:1, :], 0.0) + jnp.where(second, weight_f[1:2, :], 0.0)
     high = mixed.astype(bf16)
     low = (mixed - high.astype(f32)).astype(bf16)
-    fwd = values_f + from_slots(high, table_f) + from_slots(low, table_f)
+    fwd = input_f.astype(f32) + from_slots(high, table_f) + from_slots(low, table_f)
     fwd_next = passed_along(fwd.astype(bf16), "pipe", 1)
 
     first, second = masks(slots_b, count * CAP)
     scaled = scaling * from_slots((first | second).astype(bf16), table_b)
+    values_b = input_b.astype(f32)
     inner = jnp.mean(values_b * scaled, axis=-1, keepdims=True)
     grad = grad_y.astype(f32) + inverse_b * scaled
     grad = grad - values_b * (inverse_b * inverse_b * inverse_b * inner)
     grad_next = passed_along(grad.astype(bf16), "pipe", -1)
-    return (fwd_next[None], grad_next[None])
+    return (written(fwd_next)[None], grad_next[None])
 
 
 def solution(mesh):

time: 314 us -> 308 us (0.981)
  local copies, waits for them, and re-layouts: 4.99 us -> 1.13 us
    pallas_call x2 -> x3, Pallas kernels: 12.1 us -> 14.9 us  [the longest x2 12.8 us: dispatch(): pl.pallas_call(functools.partial(dispatch_kernel, grad is not None), grid...]
  transfers between devices with their start and end apart: 6 -> 6, of which waited for: 6 -> 6; matrix products, arithmetic and copies ran while one was open for 4% -> 4% of each run, Pallas kernels for 20% -> 22%
where the time goes in v3:
time: 308 us; the launch traced here: 307 us
  waiting for transfers between devices  193 us (63%)
  Pallas kernels  71.7 us (23%)
  starting transfers between devices  28.3 us (9%)
  matrix products  10.3 us (3%)
    all_to_all x4, waiting for transfers between devices, exchange(): lax.all_to_all(pieces, 'expert', split_axis=0, concat_axis=0, tiled=True)  173 us
    ppermute x2, waiting for transfers between devices, passed_along(): return lax.ppermute(value, axis, pairs)  19.7 us
    all_to_all x4, starting transfers between devices, exchange(): lax.all_to_all(pieces, 'expert', split_axis=0, concat_axis=0, tiled=True)  19.6 us
    pallas_call x1, Pallas kernels, expert_forward(): pl.pallas_call(functools.partial(forward_kernel, tiles), grid=(tiles + ou...  19.5 us
    pallas_call x1, Pallas kernels, expert_gate_grads(): pl.pallas_call(gate_grads_kernel, grid=(hid // tile,), in_specs=[ANY, pro...  14 us
    pallas_call x1, Pallas kernels, expert_entry_grads(): pl.pallas_call(entry_grads_kernel, grid=(steps,), in_specs=[whole(gate_gr...  13.7 us
    pallas_call x2, Pallas kernels, dispatch(): pl.pallas_call(functools.partial(dispatch_kernel, grad is not None), grid...  12.8 us
    dot_general x3, matrix products, from_slots(): lax.dot_general(place, table, (((0,), (0,)), ((), ())), preferred_element...  10.3 us
  transfers between devices with their start and end apart: 6, of which 6 were waited for; matrix products, arithmetic and copies ran while one was open for 4% of the time, Pallas kernels for 22%

profile of v3, /device:TPU:0, one launch (start us, length us, event | category | flops | bytes accessed | tf_op | source)
XLA Modules:
  0.0 307.0 jit_solution(5444397599347159753)
XLA Ops:
  0.6 5.5 %shard_map.131 = (bf16[16,32,4096]{2,1,0:T(8,128)(2,1)}, s32[2,128]{1,0:T(2,128)}, f32[128,1]{1,0:T(8,128)}) custom-call(s32[1,16]{1,0:T(1,128)} %quota.3, s32[2,128]{1,0:T(2,128)} %bitcast.64, f32[2,128]{1,0:T(2,128)} %bitcast.56, f32[1,4096]{1,0:T(1,128)} %scaling_ref.3, bf16[128,4096]{1,0:T(8,128)(2,1)} %bitcast.51), custom_call_target="tpu_custom_call" | custom-call | flops 536870912 | bytes 6291456 | tf_op jit(solution)/shard_map/pallas_call | solution.py:97
  6.1 5.6 %all-to-all-start = ((bf16[16,32,4096]{2,1,0:T(8,128)(2,1)}), bf16[16,32,4096]{2,1,0:T(8,128)(2,1)}, u32[]{:S(2)}, u32[]{:S(2)}) async-start(bf16[16,32,4096]{2,1,0:T(8,128)(2,1)} %get-tuple-element.13), calls=%async_computation | async-start | bytes 8388608 | tf_op jit(solution)/shard_map/all_to_all | solution.py:279
  11.7 7.3 %shard_map.133 = (bf16[16,64,4096]{2,1,0:T(8,128)(2,1)}, s32[2,128]{1,0:T(2,128)}, f32[128,1]{1,0:T(8,128)}) custom-call(s32[1,16]{1,0:T(1,128)} %quota.3, s32[2,128]{1,0:T(2,128)} %bitcast.65, f32[2,128]{1,0:T(2,128)} %bitcast.66, f32[1,4096]{1,0:T(1,128)} %scaling_ref.3, bf16[128,4096]{1,0:T(8,128)(2,1)} %bitcast.50, bf16[128,4096]{1,0:T(8,128)(2,1)} %bitcast.54), custom_call_target="tpu_custom_call" | custom-call | flops 1073741824 | bytes 10485760 | tf_op jit(solution)/shard_map/pallas_call | solution.py:97
  19.1 43.1 %all-to-all-done.source = bf16[16,32,4096]{2,1,0:T(8,128)(2,1)} async-done(((bf16[16,32,4096]{2,1,0:T(8,128)(2,1)}), bf16[16,32,4096]{2,1,0:T(8,128)(2,1)}, u32[]{:S(2)}, u32[]{:S(2)}) %all-to-all-start) | async-done | bytes 4194336 | tf_op jit(solution)/shard_map/all_to_all | solution.py:279
  62.2 4.8 %all-to-all-start.1 = ((bf16[16,64,4096]{2,1,0:T(8,128)(2,1)}), bf16[16,64,4096]{2,1,0:T(8,128)(2,1)}, u32[]{:S(2)}, u32[]{:S(2)}) async-start(bf16[16,64,4096]{2,1,0:T(8,128)(2,1)} %get-tuple-element.15), calls=%async_computation.1 | async-start | bytes 16777216 | tf_op jit(solution)/shard_map/all_to_all | solution.py:279
  66.9 19.5 %shard_map.132 = bf16[512,4096]{1,0:T(8,128)(2,1)} custom-call(bf16[16,32,4096]{2,1,0:T(8,128)(2,1)} %all-to-all-done.source, bf16[4096,768]{1,0:T(8,128)(2,1)} %bitcast.58, bf16[4096,768]{1,0:T(8,128)(2,1)} %bitcast.61, bf16[768,4096]{1,0:T(8,128)(2,1)} %bitcast.46), custom_call_target="tpu_custom_call" | custom-call | flops 9663676416 | bytes 27262976 | tf_op jit(solution)/shard_map/pallas_call | solution.py:170
  86.5 75.8 %all-to-all-done.1.source = bf16[16,64,4096]{2,1,0:T(8,128)(2,1)} async-done(((bf16[16,64,4096]{2,1,0:T(8,128)(2,1)}), bf16[16,64,4096]{2,1,0:T(8,128)(2,1)}, u32[]{:S(2)}, u32[]{:S(2)}) %all-to-all-start.1) | async-done | bytes 8388640 | tf_op jit(solution)/shard_map/all_to_all | solution.py:279
  162.2 4.5 %all-to-all-start.2 = ((bf16[16,32,4096]{2,1,0:T(8,128)(2,1)}), bf16[16,32,4096]{2,1,0:T(8,128)(2,1)}, u32[]{:S(2)}, u32[]{:S(2)}) async-start(bf16[16,32,4096]{2,1,0:T(8,128)(2,1)} %bitcast.49), calls=%async_computation.2 | async-start | bytes 8388608 | tf_op jit(solution)/shard_map/all_to_all | solution.py:279
  166.8 9.5 %shard_map.135.hidden_ref = f32[512,768]{1,0:T(8,128)} custom-call(bf16[16,64,4096]{2,1,0:T(8,128)(2,1)} %all-to-all-done.1.source, bf16[768,4096]{1,0:T(8,128)(2,1)} %bitcast.47), custom_call_target="tpu_custom_call" | custom-call | flops 3221225472 | bytes 10485760 | tf_op jit(solution)/shard_map/pallas_call | solution.py:203
  176.3 14.0 %shard_map.136 = (bf16[512,768]{1,0:T(8,128)(2,1)}, bf16[512,768]{1,0:T(8,128)(2,1)}) custom-call(bf16[16,64,4096]{2,1,0:T(8,128)(2,1)} %all-to-all-done.1.source, bf16[4096,768]{1,0:T(8,128)(2,1)} %bitcast.59, bf16[4096,768]{1,0:T(8,128)(2,1)} %bitcast.62, f32[512,768]{1,0:T(8,128)} %shard_map.135.hidden_ref), custom_call_target="tpu_custom_call" | custom-call | flops 6442450944 | bytes 19922944 | tf_op jit(solution)/shard_map/pallas_call | solution.py:238
  190.4 13.7 %shard_map.137 = bf16[512,4096]{1,0:T(8,128)(2,1)} custom-call(bf16[512,768]{1,0:T(8,128)(2,1)} %get-tuple-element.19.gate_grad, bf16[512,768]{1,0:T(8,128)(2,1)} %get-tuple-element.20.up_grad, bf16[4096,768]{1,0:T(8,128)(2,1)} %bitcast.60, bf16[4096,768]{1,0:T(8,128)(2,1)} %bitcast.63), custom_call_target="tpu_custom_call" | custom-call | flops 6442450944 | bytes 18350080 | tf_op jit(solution)/shard_map/pallas_call | solution.py:267
  204.1 13.1 %all-to-all-done.2 = bf16[16,32,4096]{2,1,0:T(8,128)(2,1)} async-done(((bf16[16,32,4096]{2,1,0:T(8,128)(2,1)}), bf16[16,32,4096]{2,1,0:T(8,128)(2,1)}, u32[]{:S(2)}, u32[]{:S(2)}) %all-to-all-start.2) | async-done | bytes 4194336 | tf_op jit(solution)/shard_map/all_to_all | solution.py:279
  217.2 0.0 copy-start.4
  217.2 0.0 copy-start.6
  217.2 0.0 copy-start.5
  217.2 0.0 copy-start.1
  217.2 4.7 %all-to-all-start.3 = ((bf16[16,32,4096]{2,1,0:T(8,128)(2,1)}), bf16[16,32,4096]{2,1,0:T(8,128)(2,1)}, u32[]{:S(2)}, u32[]{:S(2)}) async-start(bf16[16,32,4096]{2,1,0:T(8,128)(2,1)} %bitcast.48), calls=%async_computation.3 | async-start | bytes 8388608 | tf_op jit(solution)/shard_map/all_to_all | solution.py:279
  221.9 0.0 copy-done.4
  221.9 0.0 copy-done.6
  221.9 0.0 copy-done.5
  221.9 0.0 copy-done.1
  222.0 3.0 convolution_add_fusion.1
  224.9 0.0 copy-start
  224.9 0.0 copy-start.3
  224.9 4.1 %fusion = bf16[128,4096]{1,0:T(8,128)(2,1)} fusion(f32[128,4096]{1,0:T(8,128)S(1)} %convolution_add_fusion.1, bf16[512,4096]{1,0:T(8,128)(2,1)} %bitcast.20, f32[128]{0:T(128)S(1)} %get-tuple-element.29, s32[128]{0:T(128)S(1)} %get-tuple-element.27, f32[128]{0:T(128)S(1)} %get-tuple-element.28, s32[128]{0:T(128)S(1)} %get-tuple-element.26), kind=kOutput, calls=%fused_computation.3 | convolution fusion | flops 538509312 | bytes 7342080 | tf_op jit(solution)/shard_map/dot_general | solution.py:283
  229.0 1.9 collective-permute-start
  230.9 41.3 %all-to-all-done.3 = bf16[16,32,4096]{2,1,0:T(8,128)(2,1)} async-done(((bf16[16,32,4096]{2,1,0:T(8,128)(2,1)}), bf16[16,32,4096]{2,1,0:T(8,128)(2,1)}, u32[]{:S(2)}, u32[]{:S(2)}) %all-to-all-start.3) | async-done | bytes 4194336 | tf_op jit(solution)/shard_map/all_to_all | solution.py:279
  272.2 0.0 copy-done
  272.2 0.0 copy-done.3
  272.2 0.0 copy-start.2
  272.3 3.2 %fusion.1 = (f32[128]{0:T(128)S(1)}, f32[128,4096]{1,0:T(8,128)S(1)}) fusion(bf16[1,128,4096]{2,1,0:T(8,128)(2,1)S(1)} %copy-done, bf16[512,4096]{1,0:T(8,128)(2,1)} %bitcast.26, s32[128]{0:T(128)S(1)} %get-tuple-element.25, s32[128]{0:T(128)S(1)} %get-tuple-element.24, f32[4096]{0:T(1024)S(1)} %bitcast.55), kind=kOutput, calls=%fused_computation.6 | convolution fusion | flops 539164544 | bytes 7357952 | tf_op jit(solution)/shard_map/dot_general | solution.py:283
  275.5 0.1 copy.15
  275.6 0.0 copy-done.2
  275.6 0.1 fusion.20
  275.7 1.8 fusion.3
  277.5 6.7 %collective-permute-start.1 = (bf16[128,4096]{1,0:T(8,128)(2,1)S(1)}, bf16[128,4096]{1,0:T(8,128)(2,1)S(1)}, u32[]{:S(2)}, u32[]{:S(2)}) collective-permute-start(bf16[128,4096]{1,0:T(8,128)(2,1)S(1)} %fusion.3), channel_id=1, source_target_pairs={{0,112},{16,0},{32,16},{48,32},{64,48},{80,64},{96,80},{112,96},{1... | collective-permute-start | bytes 3145736 | tf_op jit(solution)/shard_map/ppermute | solution.py:34
  284.3 14.0 %collective-permute-done.source = bf16[128,4096]{1,0:T(8,128)(2,1)} collective-permute-done((bf16[128,4096]{1,0:T(8,128)(2,1)}, bf16[128,4096]{1,0:T(8,128)(2,1)}, u32[]{:S(2)}, u32[]{:S(2)}) %collective-permute-start) | collective-permute-done | bytes 1048608 | tf_op jit(solution)/shard_map/ppermute | solution.py:34
  298.3 2.0 shard_map.134
  300.3 5.7 %collective-permute-done.1 = bf16[128,4096]{1,0:T(8,128)(2,1)S(1)} collective-permute-done((bf16[128,4096]{1,0:T(8,128)(2,1)S(1)}, bf16[128,4096]{1,0:T(8,128)(2,1)S(1)}, u32[]{:S(2)}, u32[]{:S(2)}) %collective-permute-start.1) | collective-permute-done | bytes 1048608 | tf_op jit(solution)/shard_map/ppermute | solution.py:34
  306.0 1.0 copy.17
  (4 shorter events, 0.0 us)
Async XLA Ops:
  6.1 56.0 %all-to-all-start = ((bf16[16,32,4096]{2,1,0:T(8,128)(2,1)}), bf16[16,32,4096]{2,1,0:T(8,128)(2,1)}, u32[]{:S(2)}, u32[]{:S(2)}) async-start(bf16[16,32,4096]{2,1,0:T(8,128)(2,1)} %get-tuple-element.13), calls=%async_computation | async-start | bytes 8388608 | tf_op jit(solution)/shard_map/all_to_all | solution.py:279
  62.2 100.1 %all-to-all-start.1 = ((bf16[16,64,4096]{2,1,0:T(8,128)(2,1)}), bf16[16,64,4096]{2,1,0:T(8,128)(2,1)}, u32[]{:S(2)}, u32[]{:S(2)}) async-start(bf16[16,64,4096]{2,1,0:T(8,128)(2,1)} %get-tuple-element.15), calls=%async_computation.1 | async-start | bytes 16777216 | tf_op jit(solution)/shard_map/all_to_all | solution.py:279
  162.2 54.9 %all-to-all-start.2 = ((bf16[16,32,4096]{2,1,0:T(8,128)(2,1)}), bf16[16,32,4096]{2,1,0:T(8,128)(2,1)}, u32[]{:S(2)}, u32[]{:S(2)}) async-start(bf16[16,32,4096]{2,1,0:T(8,128)(2,1)} %bitcast.49), calls=%async_computation.2 | async-start | bytes 8388608 | tf_op jit(solution)/shard_map/all_to_all | solution.py:279
  217.2 4.7 %copy-start.4 = (f32[1,128,2]{1,2,0:T(2,128)S(1)}, f32[1,128,2]{1,2,0:T(2,128)}, u32[]{:S(2)}) copy-start(f32[1,128,2]{1,2,0:T(2,128)} %param.17) | copy-start | bytes 3076
  217.2 4.7 %copy-start.6 = (s32[2,128]{1,0:T(2,128)S(1)}, s32[2,128]{1,0:T(2,128)}, u32[]{:S(2)}) copy-start(s32[2,128]{1,0:T(2,128)} %get-tuple-element.18) | copy-start | bytes 3076
  217.2 4.8 %copy-start.5 = (s32[2,128]{1,0:T(2,128)S(1)}, s32[2,128]{1,0:T(2,128)}, u32[]{:S(2)}) copy-start(s32[2,128]{1,0:T(2,128)} %get-tuple-element.12) | copy-start | bytes 3076
  217.2 4.8 %copy-start.1 = (bf16[1,128,4096]{2,1,0:T(8,128)(2,1)S(1)}, bf16[1,128,4096]{2,1,0:T(8,128)(2,1)}, u32[]{:S(2)}) copy-start(bf16[1,128,4096]{2,1,0:T(8,128)(2,1)} %param.12) | copy-start | bytes 3145732
  217.2 55.1 %all-to-all-start.3 = ((bf16[16,32,4096]{2,1,0:T(8,128)(2,1)}), bf16[16,32,4096]{2,1,0:T(8,128)(2,1)}, u32[]{:S(2)}, u32[]{:S(2)}) async-start(bf16[16,32,4096]{2,1,0:T(8,128)(2,1)} %bitcast.48), calls=%async_computation.3 | async-start | bytes 8388608 | tf_op jit(solution)/shard_map/all_to_all | solution.py:279
  224.9 47.3 %copy-start = (bf16[1,128,4096]{2,1,0:T(8,128)(2,1)S(1)}, bf16[1,128,4096]{2,1,0:T(8,128)(2,1)}, u32[]{:S(2)}) copy-start(bf16[1,128,4096]{2,1,0:T(8,128)(2,1)} %param.13) | copy-start | bytes 3145732
  224.9 47.3 %copy-start.3 = (f32[1,4096]{1,0:T(1,128)S(1)}, f32[1,4096]{1,0:T(1,128)}, u32[]{:S(2)}) copy-start(f32[1,4096]{1,0:T(1,128)} %scaling_ref.3) | copy-start | bytes 49156
  229.0 69.2 %collective-permute-start = (bf16[128,4096]{1,0:T(8,128)(2,1)}, bf16[128,4096]{1,0:T(8,128)(2,1)}, u32[]{:S(2)}, u32[]{:S(2)}) collective-permute-start(bf16[128,4096]{1,0:T(8,128)(2,1)} %fusion), channel_id=1, source_target_pairs={{0,16},{16,32},{32,48},{48,64},{64,80},{80,96},{96,112},{112,0},{1... | collective-permute-start | bytes 3145736 | tf_op jit(solution)/shard_map/ppermute | solution.py:34
  272.2 3.4 %copy-start.2 = (f32[128,1]{1,0:T(8,128)S(1)}, f32[128,1]{1,0:T(8,128)}, u32[]{:S(2)}) copy-start(f32[128,1]{1,0:T(8,128)} %get-tuple-element.17) | copy-start | bytes 1540
  277.5 28.5 %collective-permute-start.1 = (bf16[128,4096]{1,0:T(8,128)(2,1)S(1)}, bf16[128,4096]{1,0:T(8,128)(2,1)S(1)}, u32[]{:S(2)}, u32[]{:S(2)}) collective-permute-start(bf16[128,4096]{1,0:T(8,128)(2,1)S(1)} %fusion.3), channel_id=1, source_target_pairs={{0,112},{16,0},{32,16},{48,32},{64,48},{80,64},{96,80},{112,96},{1... | collective-permute-start | bytes 3145736 | tf_op jit(solution)/shard_map/ppermute | solution.py:34

commit v4 on v3

--- a/solution.py
+++ b/solution.py
@@ -63,7 +63,7 @@
 
 
 def dispatch_kernel(has_grad, quota, chosen_ref, weight_ref, scaling_ref, values_ref, *refs):
-    grad_ref, (out, place_ref, inverse_ref) = refs[0], refs[-3:]
+    grad_ref, (out, place_ref, inverse_ref, chosen, scale) = refs[0], refs[-5:]
     count, _, tile = out.shape
     step = pl.program_id(0)
 
@@ -74,24 +74,25 @@
         first, second = slots_of(chosen_ref[...], quota, count)
         place_ref[0:1, :] = first
         place_ref[1:2, :] = second
-
-    first, second = masks(place_ref[...], count * CAP)
-    chosen = jnp.where(first | second, 1.0, 0.0).astype(bf16)
+        first, second = masks(place_ref[...], count * CAP)
+        chosen[...] = jnp.where(first | second, 1.0, 0.0).astype(bf16)
+        if has_grad:
+            weight = weight_ref[...]
+            mixed = jnp.where(first, weight[0:1, :], 0.0) + jnp.where(second, weight[1:2, :], 0.0)
+            scale[...] = jnp.sum(mixed, axis=1, keepdims=True)
+
     values = values_ref[:, pl.ds(pl.multiple_of(step * tile, tile), tile)].astype(f32)
     normed = (values * inverse_ref[...] * scaling_ref[...]).astype(bf16)
-    rows = jnp.dot(chosen, normed, preferred_element_type=f32)
+    rows = jnp.dot(chosen[...], normed, preferred_element_type=f32)
     out[:, :CAP, :] = rows.astype(bf16).reshape(count, CAP, tile)
     if has_grad:
-        weight = weight_ref[...]
-        scale = jnp.where(first, weight[0:1, :], 0.0) + jnp.where(second, weight[1:2, :], 0.0)
-        rows = jnp.dot(chosen, grad_ref[...], preferred_element_type=f32)
-        rows = rows * jnp.sum(scale, axis=1, keepdims=True)
+        rows = jnp.dot(chosen[...], grad_ref[...], preferred_element_type=f32) * scale[...]
         out[:, CAP:, :] = rows.astype(bf16).reshape(count, CAP, tile)
 
 
 def dispatch(quota, chosen, weight, scaling, values, grad=None):
     count, (tokens, width) = quota.shape[1], values.shape
-    tile = 1024
+    tile = 2048 if grad is None else 1024
     rows_each = CAP if grad is None else 2 * CAP
     column = pl.BlockSpec((tokens, tile), lambda i: (0, i))
     return pl.pallas_call(
@@ -114,6 +115,10 @@
             jax.ShapeDtypeStruct((count, rows_each, width), bf16),
             jax.ShapeDtypeStruct(chosen.shape, jnp.int32),
             jax.ShapeDtypeStruct((tokens, 1), f32),
+        ],
+        scratch_shapes=[
+            pltpu.VMEM((count * CAP, tokens), bf16),
+            pltpu.VMEM((count * CAP, 1), f32),
         ],
         compiler_params=params(1),
         cost_estimate=cost(2 * count * rows_each * tokens * width, 2 * (count * rows_each + 2 * tokens) * width),

time: 308 us -> 307 us (level)
  no operation moved by 1% of the time
where the time goes in v4:
time: 307 us; the launch traced here: 306 us
  waiting for transfers between devices  193 us (63%)
  Pallas kernels  70.9 us (23%)
  starting transfers between devices  28.3 us (9%)
  matrix products  10.3 us (3%)
    all_to_all x4, waiting for transfers between devices, exchange(): lax.all_to_all(pieces, 'expert', split_axis=0, concat_axis=0, tiled=True)  173 us
    ppermute x2, waiting for transfers between devices, passed_along(): return lax.ppermute(value, axis, pairs)  19.7 us
    all_to_all x4, starting transfers between devices, exchange(): lax.all_to_all(pieces, 'expert', split_axis=0, concat_axis=0, tiled=True)  19.6 us
    pallas_call x1, Pallas kernels, expert_forward(): pl.pallas_call(functools.partial(forward_kernel, tiles), grid=(tiles + ou...  19.5 us
    pallas_call x1, Pallas kernels, expert_gate_grads(): pl.pallas_call(gate_grads_kernel, grid=(hid // tile,), in_specs=[ANY, pro...  14 us
    pallas_call x1, Pallas kernels, expert_entry_grads(): pl.pallas_call(entry_grads_kernel, grid=(steps,), in_specs=[whole(gate_gr...  13.7 us
    pallas_call x2, Pallas kernels, dispatch(): pl.pallas_call(functools.partial(dispatch_kernel, grad is not None), grid...  12.1 us
    dot_general x3, matrix products, from_slots(): lax.dot_general(place, table, (((0,), (0,)), ((), ())), preferred_element...  10.3 us
  transfers between devices with their start and end apart: 6, of which 6 were waited for; matrix products, arithmetic and copies ran while one was open for 4% of the time, Pallas kernels for 22%

profile of v4, /device:TPU:0, one launch (start us, length us, event | category | flops | bytes accessed | tf_op | source)
XLA Modules:
  0.0 306.2 jit_solution(12649631240528595571)
XLA Ops:
  0.6 4.7 %shard_map.131 = (bf16[16,32,4096]{2,1,0:T(8,128)(2,1)}, s32[2,128]{1,0:T(2,128)}, f32[128,1]{1,0:T(8,128)}) custom-call(s32[1,16]{1,0:T(1,128)} %quota.3, s32[2,128]{1,0:T(2,128)} %bitcast.64, f32[2,128]{1,0:T(2,128)} %bitcast.56, f32[1,4096]{1,0:T(1,128)} %scaling_ref.3, bf16[128,4096]{1,0:T(8,128)(2,1)} %bitcast.51), custom_call_target="tpu_custom_call" | custom-call | flops 536870912 | bytes 6291456 | tf_op jit(solution)/shard_map/pallas_call | solution.py:98
  5.3 5.6 %all-to-all-start = ((bf16[16,32,4096]{2,1,0:T(8,128)(2,1)}), bf16[16,32,4096]{2,1,0:T(8,128)(2,1)}, u32[]{:S(2)}, u32[]{:S(2)}) async-start(bf16[16,32,4096]{2,1,0:T(8,128)(2,1)} %get-tuple-element.13), calls=%async_computation | async-start | bytes 8388608 | tf_op jit(solution)/shard_map/all_to_all | solution.py:284
  10.9 7.4 %shard_map.133 = (bf16[16,64,4096]{2,1,0:T(8,128)(2,1)}, s32[2,128]{1,0:T(2,128)}, f32[128,1]{1,0:T(8,128)}) custom-call(s32[1,16]{1,0:T(1,128)} %quota.3, s32[2,128]{1,0:T(2,128)} %bitcast.65, f32[2,128]{1,0:T(2,128)} %bitcast.66, f32[1,4096]{1,0:T(1,128)} %scaling_ref.3, bf16[128,4096]{1,0:T(8,128)(2,1)} %bitcast.50, bf16[128,4096]{1,0:T(8,128)(2,1)} %bitcast.54), custom_call_target="tpu_custom_call" | custom-call | flops 1073741824 | bytes 10485760 | tf_op jit(solution)/shard_map/pallas_call | solution.py:98
  18.3 43.0 %all-to-all-done.source = bf16[16,32,4096]{2,1,0:T(8,128)(2,1)} async-done(((bf16[16,32,4096]{2,1,0:T(8,128)(2,1)}), bf16[16,32,4096]{2,1,0:T(8,128)(2,1)}, u32[]{:S(2)}, u32[]{:S(2)}) %all-to-all-start) | async-done | bytes 4194336 | tf_op jit(solution)/shard_map/all_to_all | solution.py:284
  61.3 4.8 %all-to-all-start.1 = ((bf16[16,64,4096]{2,1,0:T(8,128)(2,1)}), bf16[16,64,4096]{2,1,0:T(8,128)(2,1)}, u32[]{:S(2)}, u32[]{:S(2)}) async-start(bf16[16,64,4096]{2,1,0:T(8,128)(2,1)} %get-tuple-element.15), calls=%async_computation.1 | async-start | bytes 16777216 | tf_op jit(solution)/shard_map/all_to_all | solution.py:284
  66.1 19.5 %shard_map.132 = bf16[512,4096]{1,0:T(8,128)(2,1)} custom-call(bf16[16,32,4096]{2,1,0:T(8,128)(2,1)} %all-to-all-done.source, bf16[4096,768]{1,0:T(8,128)(2,1)} %bitcast.58, bf16[4096,768]{1,0:T(8,128)(2,1)} %bitcast.61, bf16[768,4096]{1,0:T(8,128)(2,1)} %bitcast.46), custom_call_target="tpu_custom_call" | custom-call | flops 9663676416 | bytes 27262976 | tf_op jit(solution)/shard_map/pallas_call | solution.py:175
  85.7 75.8 %all-to-all-done.1.source = bf16[16,64,4096]{2,1,0:T(8,128)(2,1)} async-done(((bf16[16,64,4096]{2,1,0:T(8,128)(2,1)}), bf16[16,64,4096]{2,1,0:T(8,128)(2,1)}, u32[]{:S(2)}, u32[]{:S(2)}) %all-to-all-start.1) | async-done | bytes 8388640 | tf_op jit(solution)/shard_map/all_to_all | solution.py:284
  161.4 4.5 %all-to-all-start.2 = ((bf16[16,32,4096]{2,1,0:T(8,128)(2,1)}), bf16[16,32,4096]{2,1,0:T(8,128)(2,1)}, u32[]{:S(2)}, u32[]{:S(2)}) async-start(bf16[16,32,4096]{2,1,0:T(8,128)(2,1)} %bitcast.49), calls=%async_computation.2 | async-start | bytes 8388608 | tf_op jit(solution)/shard_map/all_to_all | solution.py:284
  166.0 9.5 %shard_map.135.hidden_ref = f32[512,768]{1,0:T(8,128)} custom-call(bf16[16,64,4096]{2,1,0:T(8,128)(2,1)} %all-to-all-done.1.source, bf16[768,4096]{1,0:T(8,128)(2,1)} %bitcast.47), custom_call_target="tpu_custom_call" | custom-call | flops 3221225472 | bytes 10485760 | tf_op jit(solution)/shard_map/pallas_call | solution.py:208
  175.5 14.0 %shard_map.136 = (bf16[512,768]{1,0:T(8,128)(2,1)}, bf16[512,768]{1,0:T(8,128)(2,1)}) custom-call(bf16[16,64,4096]{2,1,0:T(8,128)(2,1)} %all-to-all-done.1.source, bf16[4096,768]{1,0:T(8,128)(2,1)} %bitcast.59, bf16[4096,768]{1,0:T(8,128)(2,1)} %bitcast.62, f32[512,768]{1,0:T(8,128)} %shard_map.135.hidden_ref), custom_call_target="tpu_custom_call" | custom-call | flops 6442450944 | bytes 19922944 | tf_op jit(solution)/shard_map/pallas_call | solution.py:243
  189.6 13.7 %shard_map.137 = bf16[512,4096]{1,0:T(8,128)(2,1)} custom-call(bf16[512,768]{1,0:T(8,128)(2,1)} %get-tuple-element.19.gate_grad, bf16[512,768]{1,0:T(8,128)(2,1)} %get-tuple-element.20.up_grad, bf16[4096,768]{1,0:T(8,128)(2,1)} %bitcast.60, bf16[4096,768]{1,0:T(8,128)(2,1)} %bitcast.63), custom_call_target="tpu_custom_call" | custom-call | flops 6442450944 | bytes 18350080 | tf_op jit(solution)/shard_map/pallas_call | solution.py:272
  203.3 13.1 %all-to-all-done.2 = bf16[16,32,4096]{2,1,0:T(8,128)(2,1)} async-done(((bf16[16,32,4096]{2,1,0:T(8,128)(2,1)}), bf16[16,32,4096]{2,1,0:T(8,128)(2,1)}, u32[]{:S(2)}, u32[]{:S(2)}) %all-to-all-start.2) | async-done | bytes 4194336 | tf_op jit(solution)/shard_map/all_to_all | solution.py:284
  216.3 0.0 copy-start.4
  216.4 0.0 copy-start.6
  216.4 0.0 copy-start.5
  216.4 0.0 copy-start.1
  216.4 4.7 %all-to-all-start.3 = ((bf16[16,32,4096]{2,1,0:T(8,128)(2,1)}), bf16[16,32,4096]{2,1,0:T(8,128)(2,1)}, u32[]{:S(2)}, u32[]{:S(2)}) async-start(bf16[16,32,4096]{2,1,0:T(8,128)(2,1)} %bitcast.48), calls=%async_computation.3 | async-start | bytes 8388608 | tf_op jit(solution)/shard_map/all_to_all | solution.py:284
  221.1 0.0 copy-done.4
  221.1 0.0 copy-done.6
  221.1 0.0 copy-done.5
  221.1 0.0 copy-done.1
  221.1 3.0 convolution_add_fusion.1
  224.1 0.0 copy-start
  224.1 0.0 copy-start.3
  224.1 4.1 %fusion = bf16[128,4096]{1,0:T(8,128)(2,1)} fusion(f32[128,4096]{1,0:T(8,128)S(1)} %convolution_add_fusion.1, bf16[512,4096]{1,0:T(8,128)(2,1)} %bitcast.20, f32[128]{0:T(128)S(1)} %get-tuple-element.29, s32[128]{0:T(128)S(1)} %get-tuple-element.27, f32[128]{0:T(128)S(1)} %get-tuple-element.28, s32[128]{0:T(128)S(1)} %get-tuple-element.26), kind=kOutput, calls=%fused_computation.3 | convolution fusion | flops 538509312 | bytes 7342080 | tf_op jit(solution)/shard_map/dot_general | solution.py:288
  228.2 1.9 collective-permute-start
  230.1 41.3 %all-to-all-done.3 = bf16[16,32,4096]{2,1,0:T(8,128)(2,1)} async-done(((bf16[16,32,4096]{2,1,0:T(8,128)(2,1)}), bf16[16,32,4096]{2,1,0:T(8,128)(2,1)}, u32[]{:S(2)}, u32[]{:S(2)}) %all-to-all-start.3) | async-done | bytes 4194336 | tf_op jit(solution)/shard_map/all_to_all | solution.py:284
  271.4 0.0 copy-done
  271.4 0.0 copy-done.3
  271.4 0.0 copy-start.2
  271.4 3.2 %fusion.1 = (f32[128]{0:T(128)S(1)}, f32[128,4096]{1,0:T(8,128)S(1)}) fusion(bf16[1,128,4096]{2,1,0:T(8,128)(2,1)S(1)} %copy-done, bf16[512,4096]{1,0:T(8,128)(2,1)} %bitcast.26, s32[128]{0:T(128)S(1)} %get-tuple-element.25, s32[128]{0:T(128)S(1)} %get-tuple-element.24, f32[4096]{0:T(1024)S(1)} %bitcast.55), kind=kOutput, calls=%fused_computation.6 | convolution fusion | flops 539164544 | bytes 7357952 | tf_op jit(solution)/shard_map/dot_general | solution.py:288
  274.7 0.1 copy.15
  274.8 0.0 copy-done.2
  274.8 0.1 fusion.20
  274.9 1.8 fusion.3
  276.7 6.7 %collective-permute-start.1 = (bf16[128,4096]{1,0:T(8,128)(2,1)S(1)}, bf16[128,4096]{1,0:T(8,128)(2,1)S(1)}, u32[]{:S(2)}, u32[]{:S(2)}) collective-permute-start(bf16[128,4096]{1,0:T(8,128)(2,1)S(1)} %fusion.3), channel_id=1, source_target_pairs={{0,112},{16,0},{32,16},{48,32},{64,48},{80,64},{96,80},{112,96},{1... | collective-permute-start | bytes 3145736 | tf_op jit(solution)/shard_map/ppermute | solution.py:34
  283.5 14.0 %collective-permute-done.source = bf16[128,4096]{1,0:T(8,128)(2,1)} collective-permute-done((bf16[128,4096]{1,0:T(8,128)(2,1)}, bf16[128,4096]{1,0:T(8,128)(2,1)}, u32[]{:S(2)}, u32[]{:S(2)}) %collective-permute-start) | collective-permute-done | bytes 1048608 | tf_op jit(solution)/shard_map/ppermute | solution.py:34
  297.5 2.0 shard_map.134
  299.5 5.7 %collective-permute-done.1 = bf16[128,4096]{1,0:T(8,128)(2,1)S(1)} collective-permute-done((bf16[128,4096]{1,0:T(8,128)(2,1)S(1)}, bf16[128,4096]{1,0:T(8,128)(2,1)S(1)}, u32[]{:S(2)}, u32[]{:S(2)}) %collective-permute-start.1) | collective-permute-done | bytes 1048608 | tf_op jit(solution)/shard_map/ppermute | solution.py:34
  305.2 1.0 copy.17
  (4 shorter events, 0.0 us)
Async XLA Ops:
  5.3 56.0 %all-to-all-start = ((bf16[16,32,4096]{2,1,0:T(8,128)(2,1)}), bf16[16,32,4096]{2,1,0:T(8,128)(2,1)}, u32[]{:S(2)}, u32[]{:S(2)}) async-start(bf16[16,32,4096]{2,1,0:T(8,128)(2,1)} %get-tuple-element.13), calls=%async_computation | async-start | bytes 8388608 | tf_op jit(solution)/shard_map/all_to_all | solution.py:284
  61.3 100.1 %all-to-all-start.1 = ((bf16[16,64,4096]{2,1,0:T(8,128)(2,1)}), bf16[16,64,4096]{2,1,0:T(8,128)(2,1)}, u32[]{:S(2)}, u32[]{:S(2)}) async-start(bf16[16,64,4096]{2,1,0:T(8,128)(2,1)} %get-tuple-element.15), calls=%async_computation.1 | async-start | bytes 16777216 | tf_op jit(solution)/shard_map/all_to_all | solution.py:284
  161.4 54.9 %all-to-all-start.2 = ((bf16[16,32,4096]{2,1,0:T(8,128)(2,1)}), bf16[16,32,4096]{2,1,0:T(8,128)(2,1)}, u32[]{:S(2)}, u32[]{:S(2)}) async-start(bf16[16,32,4096]{2,1,0:T(8,128)(2,1)} %bitcast.49), calls=%async_computation.2 | async-start | bytes 8388608 | tf_op jit(solution)/shard_map/all_to_all | solution.py:284
  216.3 4.7 %copy-start.4 = (f32[1,128,2]{1,2,0:T(2,128)S(1)}, f32[1,128,2]{1,2,0:T(2,128)}, u32[]{:S(2)}) copy-start(f32[1,128,2]{1,2,0:T(2,128)} %param.17) | copy-start | bytes 3076
  216.4 4.7 %copy-start.6 = (s32[2,128]{1,0:T(2,128)S(1)}, s32[2,128]{1,0:T(2,128)}, u32[]{:S(2)}) copy-start(s32[2,128]{1,0:T(2,128)} %get-tuple-element.18) | copy-start | bytes 3076
  216.4 4.8 %copy-start.5 = (s32[2,128]{1,0:T(2,128)S(1)}, s32[2,128]{1,0:T(2,128)}, u32[]{:S(2)}) copy-start(s32[2,128]{1,0:T(2,128)} %get-tuple-element.12) | copy-start | bytes 3076
  216.4 4.8 %copy-start.1 = (bf16[1,128,4096]{2,1,0:T(8,128)(2,1)S(1)}, bf16[1,128,4096]{2,1,0:T(8,128)(2,1)}, u32[]{:S(2)}) copy-start(bf16[1,128,4096]{2,1,0:T(8,128)(2,1)} %param.12) | copy-start | bytes 3145732
  216.4 55.1 %all-to-all-start.3 = ((bf16[16,32,4096]{2,1,0:T(8,128)(2,1)}), bf16[16,32,4096]{2,1,0:T(8,128)(2,1)}, u32[]{:S(2)}, u32[]{:S(2)}) async-start(bf16[16,32,4096]{2,1,0:T(8,128)(2,1)} %bitcast.48), calls=%async_computation.3 | async-start | bytes 8388608 | tf_op jit(solution)/shard_map/all_to_all | solution.py:284
  224.1 47.3 %copy-start = (bf16[1,128,4096]{2,1,0:T(8,128)(2,1)S(1)}, bf16[1,128,4096]{2,1,0:T(8,128)(2,1)}, u32[]{:S(2)}) copy-start(bf16[1,128,4096]{2,1,0:T(8,128)(2,1)} %param.13) | copy-start | bytes 3145732
  224.1 47.3 %copy-start.3 = (f32[1,4096]{1,0:T(1,128)S(1)}, f32[1,4096]{1,0:T(1,128)}, u32[]{:S(2)}) copy-start(f32[1,4096]{1,0:T(1,128)} %scaling_ref.3) | copy-start | bytes 49156
  228.2 69.3 %collective-permute-start = (bf16[128,4096]{1,0:T(8,128)(2,1)}, bf16[128,4096]{1,0:T(8,128)(2,1)}, u32[]{:S(2)}, u32[]{:S(2)}) collective-permute-start(bf16[128,4096]{1,0:T(8,128)(2,1)} %fusion), channel_id=1, source_target_pairs={{0,16},{16,32},{32,48},{48,64},{64,80},{80,96},{96,112},{112,0},{1... | collective-permute-start | bytes 3145736 | tf_op jit(solution)/shard_map/ppermute | solution.py:34
  271.4 3.4 %copy-start.2 = (f32[128,1]{1,0:T(8,128)S(1)}, f32[128,1]{1,0:T(8,128)}, u32[]{:S(2)}) copy-start(f32[128,1]{1,0:T(8,128)} %get-tuple-element.17) | copy-start | bytes 1540
  276.7 28.5 %collective-permute-start.1 = (bf16[128,4096]{1,0:T(8,128)(2,1)S(1)}, bf16[128,4096]{1,0:T(8,128)(2,1)S(1)}, u32[]{:S(2)}, u32[]{:S(2)}) collective-permute-start(bf16[128,4096]{1,0:T(8,128)(2,1)S(1)} %fusion.3), channel_id=1, source_target_pairs={{0,112},{16,0},{32,16},{48,32},{64,48},{80,64},{96,80},{112,96},{1... | collective-permute-start | bytes 3145736 | tf_op jit(solution)/shard_map/ppermute | solution.py:34

commit v5 on v3

--- a/solution.py
+++ b/solution.py
@@ -281,6 +281,42 @@
 
 def from_slots(place, table):
     return lax.dot_general(place, table, (((0,), (0,)), ((), ())), preferred_element_type=f32)
+
+
+def input_grads_kernel(place, inverse_ref, scaling_ref, values_ref, grad_ref, table, out, scaled):
+    step, tile = pl.program_id(0), table.shape[1]
+    span = pl.ds(pl.multiple_of(step * tile, tile), tile)
+    sums = jnp.dot(place[...], table[...], preferred_element_type=f32)
+    scaled[:, span] = scaling_ref[:, span] * sums
+
+    @pl.when(step == pl.num_programs(0) - 1)
+    def _():
+        values, inverse = values_ref[...].astype(f32), inverse_ref[...]
+        inner = jnp.mean(values * scaled[...], axis=1, keepdims=True)
+        result = grad_ref[...].astype(f32) + inverse * scaled[...]
+        out[...] = (result - values * (inverse * inverse * inverse * inner)).astype(bf16)
+
+
+def input_grads(place, inverse, scaling, values, grad, table):
+    tokens, width = values.shape
+    tile = 1024
+    return pl.pallas_call(
+        input_grads_kernel,
+        grid=(width // tile,),
+        in_specs=[
+            whole(place.shape),
+            whole(inverse.shape),
+            whole(scaling.shape),
+            whole(values.shape),
+            whole(grad.shape),
+            pl.BlockSpec((table.shape[0], tile), lambda i: (0, i)),
+        ],
+        out_specs=whole((tokens, width)),
+        out_shape=jax.ShapeDtypeStruct((tokens, width), bf16),
+        scratch_shapes=[pltpu.VMEM((tokens, width), f32)],
+        compiler_params=params(1),
+        cost_estimate=cost(2 * tokens * table.size, 2 * table.size + 6 * tokens * width),
+    )(place, inverse, scaling, values, grad, table)
 
 
 def written_kernel(source, out):
@@ -342,13 +378,10 @@
     fwd = input_f.astype(f32) + from_slots(high, table_f) + from_slots(low, table_f)
     fwd_next = passed_along(fwd.astype(bf16), "pipe", 1)
 
-    first, second = masks(slots_b, count * CAP)
-    scaled = scaling * from_slots((first | second).astype(bf16), table_b)
-    values_b = input_b.astype(f32)
-    inner = jnp.mean(values_b * scaled, axis=-1, keepdims=True)
-    grad = grad_y.astype(f32) + inverse_b * scaled
-    grad = grad - values_b * (inverse_b * inverse_b * inverse_b * inner)
-    grad_next = passed_along(grad.astype(bf16), "pipe", -1)
+    slot = lax.broadcasted_iota(jnp.int32, (input_b.shape[0], count * CAP), 1)
+    place = ((slot == slots_b[0][:, None]) | (slot == slots_b[1][:, None])).astype(bf16)
+    grad = input_grads(after(place, table_f), inverse_b, scaling, input_b, grad_y, table_b)
+    grad_next = passed_along(grad, "pipe", -1)
     return (written(fwd_next)[None], grad_next[None])
 
 

time: 308 us -> 309 us (level)
  Pallas kernels: 71.7 us -> 77.6 us
  matrix products: 10.3 us -> 5.97 us
    pallas_call x0 -> x1, Pallas kernels: none -> 5.98 us  [input_grads(): pl.pallas_call(input_grads_kernel, grid=(width // tile,), in_specs=[whole...]
    dot_general x3 -> x2, matrix products: 10.3 us -> 5.97 us  [from_slots(): lax.dot_general(place, table, (((0,), (0,)), ((), ())), preferred_element...]
  transfers between devices with their start and end apart: 6 -> 6, of which waited for: 6 -> 6; matrix products, arithmetic and copies ran while one was open for 4% -> 2% of each run, Pallas kernels for 22% -> 23%
where the time goes in v5:
time: 309 us; the launch traced here: 308 us
  waiting for transfers between devices  193 us (62%)
  Pallas kernels  77.6 us (25%)
  starting transfers between devices  28.4 us (9%)
  matrix products  5.97 us (2%)
    all_to_all x4, waiting for transfers between devices, exchange(): lax.all_to_all(pieces, 'expert', split_axis=0, concat_axis=0, tiled=True)  173 us
    all_to_all x4, starting transfers between devices, exchange(): lax.all_to_all(pieces, 'expert', split_axis=0, concat_axis=0, tiled=True)  19.7 us
    pallas_call x1, Pallas kernels, expert_forward(): pl.pallas_call(functools.partial(forward_kernel, tiles), grid=(tiles + ou...  19.5 us
    ppermute x2, waiting for transfers between devices, passed_along(): return lax.ppermute(value, axis, pairs)  19.1 us
    pallas_call x1, Pallas kernels, expert_gate_grads(): pl.pallas_call(gate_grads_kernel, grid=(hid // tile,), in_specs=[ANY, pro...  14 us
    pallas_call x1, Pallas kernels, expert_entry_grads(): pl.pallas_call(entry_grads_kernel, grid=(steps,), in_specs=[whole(gate_gr...  13.7 us
    pallas_call x2, Pallas kernels, dispatch(): pl.pallas_call(functools.partial(dispatch_kernel, grad is not None), grid...  12.8 us
    pallas_call x1, Pallas kernels, expert_hidden_grad(): pl.pallas_call(hidden_grad_kernel, grid=(hid // tile,), in_specs=[ANY, pl...  9.54 us
  transfers between devices with their start and end apart: 6, of which 6 were waited for; matrix products, arithmetic and copies ran while one was open for 2% of the time, Pallas kernels for 23%

profile of v5, /device:TPU:0, one launch (start us, length us, event | category | flops | bytes accessed | tf_op | source)
XLA Modules:
  0.0 308.0 jit_solution(2023136285369406442)
XLA Ops:
  0.6 5.5 %shard_map.131 = (bf16[16,32,4096]{2,1,0:T(8,128)(2,1)}, s32[2,128]{1,0:T(2,128)}, f32[128,1]{1,0:T(8,128)}) custom-call(s32[1,16]{1,0:T(1,128)} %quota.3, s32[2,128]{1,0:T(2,128)} %bitcast.58, f32[2,128]{1,0:T(2,128)} %bitcast.50, f32[1,4096]{1,0:T(1,128)} %scaling_ref.5, bf16[128,4096]{1,0:T(8,128)(2,1)} %bitcast.43), custom_call_target="tpu_custom_call" | custom-call | flops 536870912 | bytes 6291456 | tf_op jit(solution)/shard_map/pallas_call | solution.py:97
  6.1 5.6 %all-to-all-start = ((bf16[16,32,4096]{2,1,0:T(8,128)(2,1)}), bf16[16,32,4096]{2,1,0:T(8,128)(2,1)}, u32[]{:S(2)}, u32[]{:S(2)}) async-start(bf16[16,32,4096]{2,1,0:T(8,128)(2,1)} %get-tuple-element.14), calls=%async_computation | async-start | bytes 8388608 | tf_op jit(solution)/shard_map/all_to_all | solution.py:279
  11.7 7.3 %shard_map.133 = (bf16[16,64,4096]{2,1,0:T(8,128)(2,1)}, s32[2,128]{1,0:T(2,128)}, f32[128,1]{1,0:T(8,128)}) custom-call(s32[1,16]{1,0:T(1,128)} %quota.3, s32[2,128]{1,0:T(2,128)} %bitcast.59, f32[2,128]{1,0:T(2,128)} %bitcast.60, f32[1,4096]{1,0:T(1,128)} %scaling_ref.5, bf16[128,4096]{1,0:T(8,128)(2,1)} %bitcast.44, bf16[128,4096]{1,0:T(8,128)(2,1)} %bitcast.46), custom_call_target="tpu_custom_call" | custom-call | flops 1073741824 | bytes 10485760 | tf_op jit(solution)/shard_map/pallas_call | solution.py:97
  19.1 43.1 %all-to-all-done.source = bf16[16,32,4096]{2,1,0:T(8,128)(2,1)} async-done(((bf16[16,32,4096]{2,1,0:T(8,128)(2,1)}), bf16[16,32,4096]{2,1,0:T(8,128)(2,1)}, u32[]{:S(2)}, u32[]{:S(2)}) %all-to-all-start) | async-done | bytes 4194336 | tf_op jit(solution)/shard_map/all_to_all | solution.py:279
  62.1 4.8 %all-to-all-start.1 = ((bf16[16,64,4096]{2,1,0:T(8,128)(2,1)}), bf16[16,64,4096]{2,1,0:T(8,128)(2,1)}, u32[]{:S(2)}, u32[]{:S(2)}) async-start(bf16[16,64,4096]{2,1,0:T(8,128)(2,1)} %get-tuple-element.16), calls=%async_computation.1 | async-start | bytes 16777216 | tf_op jit(solution)/shard_map/all_to_all | solution.py:279
  67.0 19.5 %shard_map.132 = bf16[512,4096]{1,0:T(8,128)(2,1)} custom-call(bf16[16,32,4096]{2,1,0:T(8,128)(2,1)} %all-to-all-done.source, bf16[4096,768]{1,0:T(8,128)(2,1)} %bitcast.52, bf16[4096,768]{1,0:T(8,128)(2,1)} %bitcast.55, bf16[768,4096]{1,0:T(8,128)(2,1)} %bitcast.39), custom_call_target="tpu_custom_call" | custom-call | flops 9663676416 | bytes 27262976 | tf_op jit(solution)/shard_map/pallas_call | solution.py:170
  86.5 75.8 %all-to-all-done.1.source = bf16[16,64,4096]{2,1,0:T(8,128)(2,1)} async-done(((bf16[16,64,4096]{2,1,0:T(8,128)(2,1)}), bf16[16,64,4096]{2,1,0:T(8,128)(2,1)}, u32[]{:S(2)}, u32[]{:S(2)}) %all-to-all-start.1) | async-done | bytes 8388640 | tf_op jit(solution)/shard_map/all_to_all | solution.py:279
  162.3 4.5 %all-to-all-start.2 = ((bf16[16,32,4096]{2,1,0:T(8,128)(2,1)}), bf16[16,32,4096]{2,1,0:T(8,128)(2,1)}, u32[]{:S(2)}, u32[]{:S(2)}) async-start(bf16[16,32,4096]{2,1,0:T(8,128)(2,1)} %bitcast.42), calls=%async_computation.2 | async-start | bytes 8388608 | tf_op jit(solution)/shard_map/all_to_all | solution.py:279
  166.8 9.5 %shard_map.135.hidden_ref = f32[512,768]{1,0:T(8,128)} custom-call(bf16[16,64,4096]{2,1,0:T(8,128)(2,1)} %all-to-all-done.1.source, bf16[768,4096]{1,0:T(8,128)(2,1)} %bitcast.40), custom_call_target="tpu_custom_call" | custom-call | flops 3221225472 | bytes 10485760 | tf_op jit(solution)/shard_map/pallas_call | solution.py:203
  176.4 14.0 %shard_map.136 = (bf16[512,768]{1,0:T(8,128)(2,1)}, bf16[512,768]{1,0:T(8,128)(2,1)}) custom-call(bf16[16,64,4096]{2,1,0:T(8,128)(2,1)} %all-to-all-done.1.source, bf16[4096,768]{1,0:T(8,128)(2,1)} %bitcast.53, bf16[4096,768]{1,0:T(8,128)(2,1)} %bitcast.56, f32[512,768]{1,0:T(8,128)} %shard_map.135.hidden_ref), custom_call_target="tpu_custom_call" | custom-call | flops 6442450944 | bytes 19922944 | tf_op jit(solution)/shard_map/pallas_call | solution.py:238
  190.4 13.7 %shard_map.137 = bf16[512,4096]{1,0:T(8,128)(2,1)} custom-call(bf16[512,768]{1,0:T(8,128)(2,1)} %get-tuple-element.21.gate_grad, bf16[512,768]{1,0:T(8,128)(2,1)} %get-tuple-element.22.up_grad, bf16[4096,768]{1,0:T(8,128)(2,1)} %bitcast.54, bf16[4096,768]{1,0:T(8,128)(2,1)} %bitcast.57), custom_call_target="tpu_custom_call" | custom-call | flops 6442450944 | bytes 18350080 | tf_op jit(solution)/shard_map/pallas_call | solution.py:267
  204.1 13.1 %all-to-all-done.2 = bf16[16,32,4096]{2,1,0:T(8,128)(2,1)} async-done(((bf16[16,32,4096]{2,1,0:T(8,128)(2,1)}), bf16[16,32,4096]{2,1,0:T(8,128)(2,1)}, u32[]{:S(2)}, u32[]{:S(2)}) %all-to-all-start.2) | async-done | bytes 4194336 | tf_op jit(solution)/shard_map/all_to_all | solution.py:279
  217.2 0.0 copy-start.2
  217.2 0.0 copy-start.4
  217.2 0.0 copy-start.3
  217.2 0.0 copy-start
  217.2 4.7 %all-to-all-start.3 = ((bf16[16,32,4096]{2,1,0:T(8,128)(2,1)}), bf16[16,32,4096]{2,1,0:T(8,128)(2,1)}, u32[]{:S(2)}, u32[]{:S(2)}) async-start(bf16[16,32,4096]{2,1,0:T(8,128)(2,1)} %bitcast.41), calls=%async_computation.3 | async-start | bytes 8388608 | tf_op jit(solution)/shard_map/all_to_all | solution.py:279
  221.9 0.0 copy-done.2
  221.9 0.0 copy-done.4
  222.0 0.0 copy-done.3
  222.0 0.8 fusion.3.place
  222.7 0.0 copy-done
  222.8 2.9 convolution_add_fusion.1
  225.7 3.0 fusion
  228.7 2.0 collective-permute-start
  230.7 41.6 %all-to-all-done.3 = bf16[16,32,4096]{2,1,0:T(8,128)(2,1)} async-done(((bf16[16,32,4096]{2,1,0:T(8,128)(2,1)}), bf16[16,32,4096]{2,1,0:T(8,128)(2,1)}, u32[]{:S(2)}, u32[]{:S(2)}) %all-to-all-start.3) | async-done | bytes 4194336 | tf_op jit(solution)/shard_map/all_to_all | solution.py:279
  272.3 6.0 %shard_map.138 = bf16[128,4096]{1,0:T(8,128)(2,1)} custom-call(bf16[128,512]{1,0:T(8,128)(2,1)} %fusion.3.place, f32[128,1]{1,0:T(8,128)} %get-tuple-element.20.inverse_ref, f32[1,4096]{1,0:T(1,128)} %scaling_ref.5, bf16[128,4096]{1,0:T(8,128)(2,1)} %bitcast.45, bf16[128,4096]{1,0:T(8,128)(2,1)} %bitcast.47, bf16[512,4096]{1,0:T(8,128)(2,1)} %bitcast.25.table), custom_call_target="tpu_custom_call" | custom-call | flops 536870912 | bytes 7340032 | tf_op jit(solution)/shard_map/pallas_call | solution.py:303
  278.3 6.7 %collective-permute-start.1 = (bf16[128,4096]{1,0:T(8,128)(2,1)}, bf16[128,4096]{1,0:T(8,128)(2,1)S(1)}, u32[]{:S(2)}, u32[]{:S(2)}) collective-permute-start(bf16[128,4096]{1,0:T(8,128)(2,1)} %shard_map.138), channel_id=1, source_target_pairs={{0,112},{16,0},{32,16},{48,32},{64,48},{80,64},{96,80},{112,96},{1... | collective-permute-start | bytes 3145736 | tf_op jit(solution)/shard_map/ppermute | solution.py:34
  284.9 13.3 %collective-permute-done.source = bf16[128,4096]{1,0:T(8,128)(2,1)S(1)} collective-permute-done((bf16[128,4096]{1,0:T(8,128)(2,1)S(1)}, bf16[128,4096]{1,0:T(8,128)(2,1)S(1)}, u32[]{:S(2)}, u32[]{:S(2)}) %collective-permute-start) | collective-permute-done | bytes 1048608 | tf_op jit(solution)/shard_map/ppermute | solution.py:34
  298.2 0.0 copy-start.1
  298.2 1.0 copy-done.1
  299.2 2.0 shard_map.134
  301.2 5.8 %collective-permute-done.1 = bf16[128,4096]{1,0:T(8,128)(2,1)S(1)} collective-permute-done((bf16[128,4096]{1,0:T(8,128)(2,1)}, bf16[128,4096]{1,0:T(8,128)(2,1)S(1)}, u32[]{:S(2)}, u32[]{:S(2)}) %collective-permute-start.1) | collective-permute-done | bytes 1048608 | tf_op jit(solution)/shard_map/ppermute | solution.py:34
  307.0 1.0 copy.15
  (3 shorter events, 0.0 us)
Async XLA Ops:
  6.1 56.0 %all-to-all-start = ((bf16[16,32,4096]{2,1,0:T(8,128)(2,1)}), bf16[16,32,4096]{2,1,0:T(8,128)(2,1)}, u32[]{:S(2)}, u32[]{:S(2)}) async-start(bf16[16,32,4096]{2,1,0:T(8,128)(2,1)} %get-tuple-element.14), calls=%async_computation | async-start | bytes 8388608 | tf_op jit(solution)/shard_map/all_to_all | solution.py:279
  62.1 100.1 %all-to-all-start.1 = ((bf16[16,64,4096]{2,1,0:T(8,128)(2,1)}), bf16[16,64,4096]{2,1,0:T(8,128)(2,1)}, u32[]{:S(2)}, u32[]{:S(2)}) async-start(bf16[16,64,4096]{2,1,0:T(8,128)(2,1)} %get-tuple-element.16), calls=%async_computation.1 | async-start | bytes 16777216 | tf_op jit(solution)/shard_map/all_to_all | solution.py:279
  162.3 54.9 %all-to-all-start.2 = ((bf16[16,32,4096]{2,1,0:T(8,128)(2,1)}), bf16[16,32,4096]{2,1,0:T(8,128)(2,1)}, u32[]{:S(2)}, u32[]{:S(2)}) async-start(bf16[16,32,4096]{2,1,0:T(8,128)(2,1)} %bitcast.42), calls=%async_computation.2 | async-start | bytes 8388608 | tf_op jit(solution)/shard_map/all_to_all | solution.py:279
  217.2 4.7 %copy-start.2 = (f32[1,128,2]{1,2,0:T(2,128)S(1)}, f32[1,128,2]{1,2,0:T(2,128)}, u32[]{:S(2)}) copy-start(f32[1,128,2]{1,2,0:T(2,128)} %param.17) | copy-start | bytes 3076
  217.2 4.8 %copy-start.4 = (s32[2,128]{1,0:T(2,128)S(1)}, s32[2,128]{1,0:T(2,128)}, u32[]{:S(2)}) copy-start(s32[2,128]{1,0:T(2,128)} %get-tuple-element.18) | copy-start | bytes 3076
  217.2 4.8 %copy-start.3 = (s32[2,128]{1,0:T(2,128)S(1)}, s32[2,128]{1,0:T(2,128)}, u32[]{:S(2)}) copy-start(s32[2,128]{1,0:T(2,128)} %get-tuple-element.13) | copy-start | bytes 3076
  217.2 5.6 %copy-start = (bf16[1,128,4096]{2,1,0:T(8,128)(2,1)S(1)}, bf16[1,128,4096]{2,1,0:T(8,128)(2,1)}, u32[]{:S(2)}) copy-start(bf16[1,128,4096]{2,1,0:T(8,128)(2,1)} %param.12) | copy-start | bytes 3145732
  217.2 55.1 %all-to-all-start.3 = ((bf16[16,32,4096]{2,1,0:T(8,128)(2,1)}), bf16[16,32,4096]{2,1,0:T(8,128)(2,1)}, u32[]{:S(2)}, u32[]{:S(2)}) async-start(bf16[16,32,4096]{2,1,0:T(8,128)(2,1)} %bitcast.41), calls=%async_computation.3 | async-start | bytes 8388608 | tf_op jit(solution)/shard_map/all_to_all | solution.py:279
  228.7 69.5 %collective-permute-start = (bf16[128,4096]{1,0:T(8,128)(2,1)S(1)}, bf16[128,4096]{1,0:T(8,128)(2,1)S(1)}, u32[]{:S(2)}, u32[]{:S(2)}) collective-permute-start(bf16[128,4096]{1,0:T(8,128)(2,1)S(1)} %fusion), channel_id=1, source_target_pairs={{0,16},{16,32},{32,48},{48,64},{64,80},{80,96},{96,112},{112,0},{1... | collective-permute-start | bytes 3145736 | tf_op jit(solution)/shard_map/ppermute | solution.py:34
  278.3 28.7 %collective-permute-start.1 = (bf16[128,4096]{1,0:T(8,128)(2,1)}, bf16[128,4096]{1,0:T(8,128)(2,1)S(1)}, u32[]{:S(2)}, u32[]{:S(2)}) collective-permute-start(bf16[128,4096]{1,0:T(8,128)(2,1)} %shard_map.138), channel_id=1, source_target_pairs={{0,112},{16,0},{32,16},{48,32},{64,48},{80,64},{96,80},{112,96},{1... | collective-permute-start | bytes 3145736 | tf_op jit(solution)/shard_map/ppermute | solution.py:34
  298.2 1.0 copy-start.1
